TPU v7x, 32 devices: a whole 2x2x4 slice. The times are simulated.
32 devices in a mesh: ha: 8 (over z, y), ta: 2 (over x), col: 2 (over core).
Axes of the slice: x: 2, y: 2, z: 4, core: 2. Of those that a mesh axis runs over, the one named last changes fastest.
Arguments:
- tokens: bfloat16 [16, 224, 28, 128], P(('col', 'ta'), 'ha'), parts along dimension 0, may hold values from -6 to 6
- regions_one: int32 [16, 224, 28], P(('col', 'ta'), 'ha'), parts along dimension 0, may hold values from 0 to 2
- regions_three: int32 [16, 56, 7], P(('col', 'ta'), 'ha'), parts along dimension 0, may hold values from 0 to 2
- gain_one: float32 [128], replicated, may hold values from 0.25 to 1.75
- projection_one: bfloat16 [128, 384], replicated, may hold values from -0.5 to 0.5
- outward_one: bfloat16 [128, 128], replicated, may hold values from -0.5 to 0.5
- table_one: float32 [1183, 4], replicated, may hold values from -4 to 303
- merge_gain_one: float32 [512], replicated, may hold values from 0.25 to 1.75
- merge_weight_one: bfloat16 [512, 256], replicated, may hold values from -0.25 to 0.25
- merge_gain_two: float32 [1024], replicated, may hold values from 0.25 to 1.75
- merge_weight_two: bfloat16 [1024, 512], replicated, may hold values from -0.1875 to 0.1875
- gain_three: float32 [512], replicated, may hold values from 0.25 to 1.75
- projection_three: bfloat16 [512, 1536], replicated, may hold values from -0.25 to 0.25
- outward_three: bfloat16 [512, 512], replicated, may hold values from -0.25 to 0.25
- table_three: float32 [1183, 16], replicated, may hold values from -4 to 303
- cotangent: bfloat16 [16, 56, 7, 512], P(('col', 'ta'), 'ha'), parts along dimension 0, may hold values from -6 to 6
Outputs:
- section_three: bfloat16 [16, 56, 7, 512], P(('col', 'ta'), 'ha'), parts along dimension 0
- grad_tokens: bfloat16 [16, 224, 28, 128], P(('col', 'ta'), 'ha'), parts along dimension 0
There are 2 independent parts, one for each index of `col`. A program takes and returns all parts, laid end to end along the dimension named above; an argument that names none is the same for every part. Nothing has to cross between parts.
Inputs may be any that keep to these rules, and one draw needn't show every extreme that they name: `regions_one`: region ids are free for each position. `regions_three`: region ids are free for each position.
All inputs are finite; a program needn't handle non-finite values.
Results may differ from a plain program's by a relative error of at most 0.03.
Values may be sent and summed in bfloat16 or wider, within the bound.
No kernel may reach another device: no remote copies, remote signals or barrier semaphores. Data moves between devices by JAX's collectives and lax.ppermute only.
A program may use at most 192 MiB of HBM per device.

v0:
```python
import functools

import jax
import jax.numpy as jnp
import numpy as np
from jax import lax
from jax.experimental import pallas as pl
from jax.experimental.pallas import tpu as pltpu
from jax.sharding import PartitionSpec as P

HEADS1 = 4
HEADS3 = 16
WT = 4
WS = 7
ST = 2
SS = 3
EPSILON = 1e-05
LOG2E = 1.4426950408889634
HEAD = 32
SCALE = HEAD**-0.5
ROWS = WT * WS * 8
LANES = 256
SPAN = 1280
GONE = -1e30
PER_STEP = 2
STEPS = 8 // PER_STEP
BF = jnp.bfloat16
F32 = jnp.float32


def dot(a, b):
    return jnp.dot(a, b, preferred_element_type=F32)


def dot_nt(a, b):
    return lax.dot_general(a, b, (((1,), (1,)), ((), ())), preferred_element_type=F32)


def params(limit=60):
    return pltpu.CompilerParams(vmem_limit_bytes=limit * 1024 * 1024)


def normalise(x):
    centred = x - jnp.mean(x, -1, keepdims=True)
    rstd = lax.rsqrt(jnp.mean(centred * centred, -1, keepdims=True) + EPSILON)
    return centred * rstd, rstd


def normalise_back(grad, xhat, rstd):
    return rstd * (
        grad
        - jnp.mean(grad, -1, keepdims=True)
        - xhat * jnp.mean(grad * xhat, -1, keepdims=True)
    )


def head_rows(x, h):
    return x[HEAD * h : HEAD * (h + 1)]


def head_of_lane(shape):
    return lax.broadcasted_iota(jnp.int32, shape, 1) // HEAD


def by_head(x):
    lane = head_of_lane((1, 128))
    return jnp.concatenate([x * (lane == h).astype(F32).astype(BF) for h in range(4)], 0)


def pick_heads(stacked):
    lane = head_of_lane((ROWS, 128))
    got = stacked[:ROWS]
    for h in range(1, 4):
        got = jnp.where(lane == h, stacked[ROWS * h : ROWS * (h + 1)], got)
    return got


def lengthen(x):
    return jnp.concatenate([x, jnp.zeros((LANES - ROWS, x.shape[1]), x.dtype)], 0)


def region_mask(row):
    wide = jnp.broadcast_to(row.astype(F32), (128, LANES))
    column = wide.T[:ROWS]
    column = jnp.concatenate([column, column], 1)
    return jnp.where(column == wide[0:1], 0.0, GONE).astype(F32)


def attend_four(windows):
    scores = [dot(by_head(k), qT) for k, qT, _, _, _, _ in windows]
    results = []
    for s, (_, _, vT, mask, bias_at, keep_probs) in zip(scores, windows):
        outs, inverses = [], []
        for h in range(4):
            biased = s[ROWS * h : ROWS * (h + 1)] + (bias_at(h) + mask)
            peak = jnp.max(biased, 0, keepdims=True)
            probs = jnp.exp2(biased - peak).astype(BF)
            keep_probs(h, probs)
            extended = jnp.concatenate([head_rows(vT, h)[:, :ROWS], jnp.ones((16, ROWS), BF)], 0)
            out = dot(extended, probs)
            inverse = 1.0 / out[HEAD : HEAD + 1]
            outs.append(out[:HEAD] * inverse)
            inverses.append(inverse)
        results.append((jnp.concatenate(outs, 0), jnp.concatenate(inverses + inverses, 0)))
    return results


def attend_four_back(windows):
    first = []
    for v, qT, kT, oT, doT, inverse, probs_at in windows:
        scaled, deltas = [], []
        for h in range(4):
            part = head_rows(doT, h) * inverse[h : h + 1]
            deltas.append(jnp.sum(part * head_rows(oT, h), 0, keepdims=True))
            scaled.append(part)
        scaled = jnp.concatenate(scaled, 0).astype(BF)
        first.append((scaled, deltas, dot(by_head(v), scaled)))
    results = []
    for (scaled, deltas, dprobs), (v, qT, kT, oT, doT, inverse, probs_at) in zip(first, windows):
        probs = [probs_at(h) for h in range(4)]
        dscores = [
            (probs[h].astype(F32) * (dprobs[ROWS * h : ROWS * (h + 1)] - deltas[h])).astype(BF)
            for h in range(4)
        ]
        dv = pick_heads(dot_nt(jnp.concatenate(probs, 0), scaled))
        dk = pick_heads(dot_nt(jnp.concatenate(dscores, 0), qT))
        dqT = jnp.concatenate(
            [dot(head_rows(kT, h)[:, :ROWS], dscores[h]) for h in range(4)], 0
        )
        results.append((dqT.T[:ROWS] * SCALE, dk * (1.0 / LOG2E), dv))
    return results


def bias_kernel(t1_ref, t3_ref, s1_ref, s3_ref, o1_ref, o3_ref, x_ref):
    for t_ref, s_ref, o_ref, heads, section in (
        (t1_ref, s1_ref, o1_ref, HEADS1, 1),
        (t3_ref, s3_ref, o3_ref, HEADS3, 3),
    ):
        for head in range(heads):
            row = jnp.broadcast_to(t_ref[head : head + 1, :], (8, SPAN))
            turned = pltpu.roll(row, 0, 1, stride=1, stride_axis=0)
            if section == 3:
                turned = jnp.concatenate([turned[4:7], turned[0:5]], 0)
            x_ref[8 * head : 8 * head + 8, :] = turned
        chosen = s_ref[...]
        for tj in range(WT):
            rows = []
            for hj in range(WS):
                slabs = []
                for ti in range(WT):
                    start = (ti - tj + 3) * 169 + (6 - hj) * 13 + 6
                    low = start // 128 * 128
                    pair = x_ref[0 : 8 * heads, low : low + 256]
                    turn = start - low
                    slabs.append(pltpu.roll(pair, 256 - turn, 1)[:, :128] if turn else pair[:, :128])
                rows.append(jnp.concatenate(slabs, 1))
            left = jnp.concatenate(rows, 0)
            first = left.astype(BF)
            rest = left - first.astype(F32)
            second = rest.astype(BF)
            third = (rest - second.astype(F32)).astype(BF)
            got = dot(first, chosen) + dot(second, chosen) + dot(third, chosen)
            for hj in range(WS):
                for head in range(heads):
                    at = (hj * heads + head) * 8
                    o_ref[head, (tj * WS + hj) * 8 : (tj * WS + hj) * 8 + 8, :] = got[at : at + 8]


def column_order(section):
    return [(c + 4) % 7 if section == 3 else c for c in range(7)]


def chooser(section):
    chosen = np.zeros((WT * 128, LANES), np.float32)
    for ti in range(WT):
        for hi in range(WS):
            for c, wi in enumerate(column_order(section)):
                chosen[ti * 128 + 13 * hi + wi, ti * 56 + hi * 8 + c] = 1.0
    return jnp.asarray(chosen, BF)


def widen_table(table):
    return jnp.pad(jnp.transpose(table) * LOG2E, ((0, 0), (0, SPAN - table.shape[0])))


def build_biases(table_one, table_three):
    return pl.pallas_call(
        bias_kernel,
        out_shape=(
            jax.ShapeDtypeStruct((HEADS1, ROWS, LANES), F32),
            jax.ShapeDtypeStruct((HEADS3, ROWS, LANES), F32),
        ),
        scratch_shapes=[pltpu.VMEM((HEADS3 * 8, SPAN), F32)],
        compiler_params=params(),
    )(widen_table(table_one), widen_table(table_three), chooser(1), chooser(3))


def fold(values):
    return jnp.concatenate([values[..., 128 * g : 128 * g + 128] for g in range(4)], -2)


def unfold(values):
    return jnp.concatenate([values[..., 7 * g : 7 * g + 7, :] for g in range(4)], -1)


def pack_kernel(tok_ref, cot_ref, early_ref, late_ref, ha_ref, dg_ref):
    early_ref[...] = tok_ref[0:2, 3:17]
    late_ref[:, 0:11] = tok_ref[0:2, 17:28]
    late_ref[:, 11:15] = fold(cot_ref[0:2, 3:7].astype(F32)).astype(BF)
    ha_ref[:, 0:3] = tok_ref[2:4, 0:3]
    ha_ref[:, 3:6] = fold(cot_ref[2:4, 0:3].astype(F32)).astype(BF)
    dg_ref[:, 0:3] = tok_ref[0:2, 0:3]
    dg_ref[:, 3:6] = fold(cot_ref[0:2, 0:3].astype(F32)).astype(BF)


def pack(tokens, cotangent):
    return pl.pallas_call(
        pack_kernel,
        out_shape=[
            jax.ShapeDtypeStruct((2, n, 28, 128), BF) for n in (14, 15, 6, 6)
        ],
        compiler_params=params(),
    )(tokens, cotangent)


def put_rows(stage, frames, rows, values):
    values = values.astype(F32)
    stage[frames, rows, 0:28, :] = values
    stage[frames, rows, 28:36, :] = values[:, :, 0:8, :]


def cut_windows(stage, win):
    for hw in range(2):
        for ww in range(4):
            win[hw * 4 + ww] = stage[:, 7 * hw : 7 * hw + 7, 3 + 7 * ww : 11 + 7 * ww, :].reshape(
                ROWS, 128
            )


def join_windows(win, stage):
    for hw in range(2):
        for ww in range(4):
            stage[:, 7 * hw : 7 * hw + 7, 3 + 7 * ww : 11 + 7 * ww, :] = win[hw * 4 + ww].reshape(
                WT, WS, 8, 128
            )
    stage[:, :, 0:3, :] = stage[:, :, 28:31, :]


def front_kernel(late, *refs):
    n_in = 4 if late else 2
    pieces, refs = refs[:n_in], refs[n_in:]
    gain_ref, proj_ref, projT_ref, outw_ref, bias_ref, row_ref = refs[:6]
    refs = refs[6:]
    n_out = 1 if late else 2
    outs, refs = refs[:n_out], refs[n_out:]
    xw_ref, kv_ref, t_ref, p_ref, o_ref, inv_ref, stage, win = refs
    step = pl.program_id(0)

    @pl.when(step == 0)
    def _():
        own = pieces[0]
        if late:
            put_rows(stage, slice(0, 2), slice(0, 11), own[2:4, 17:28])
            put_rows(stage, slice(2, 4), slice(0, 11), pieces[1][:, 0:11])
            put_rows(stage, slice(0, 2), slice(11, 14), pieces[2][:, 0:3])
            put_rows(stage, slice(2, 4), slice(11, 14), pieces[3][:, 0:3])
        else:
            put_rows(stage, slice(0, 2), slice(0, 14), own[2:4, 3:17])
            put_rows(stage, slice(2, 4), slice(0, 14), pieces[1][...])
        cut_windows(stage, win)

    xs, operands = [], []
    for u in range(PER_STEP):
        x = win[step * PER_STEP + u]
        xs.append(x)
        xw_ref[u] = x.astype(BF)
        xhat, _ = normalise(x)
        n = (xhat * gain_ref[...]).astype(BF)
        kv = dot(n, proj_ref[:, 128:]).astype(BF)
        kv_ref[u] = kv
        t = dot_nt(projT_ref[...], lengthen(n))
        qT = (t[:128] * (SCALE * LOG2E)).astype(BF)
        rest = t[128:].astype(BF)
        t_ref[u, :128] = qT
        t_ref[u, 128:] = rest[:128]

        def keep(h, probs, u=u):
            p_ref[u, h] = probs

        operands.append(
            (kv[:, :128], qT, rest[128:], region_mask(row_ref[u]), lambda h: bias_ref[h], keep)
        )
    for u, (oT, inverse) in enumerate(attend_four(operands)):
        o_ref[u] = oT.astype(BF)
        inv_ref[u] = inverse
        mixed = dot(oT.T[:ROWS].astype(BF), outw_ref[...]).astype(BF).astype(F32)
        win[step * PER_STEP + u] = xs[u] + mixed

    @pl.when(step == STEPS - 1)
    def _():
        join_windows(win, stage)
        if late:
            outs[0][...] = stage[:, :, 0:28, :].astype(BF)
        else:
            outs[0][...] = stage[:, 0:9, 0:28, :].astype(BF)
            outs[1][...] = stage[:, 9:14, 0:28, :].astype(BF)


def whole(shape):
    return pl.BlockSpec(shape, lambda i: (0,) * len(shape))


def each(shape):
    return pl.BlockSpec((PER_STEP,) + shape, lambda i: (i,) + (0,) * len(shape))


SAVED = (
    ((ROWS, 128), BF),
    ((ROWS, 256), BF),
    ((256, LANES), BF),
    ((4, ROWS, LANES), BF),
    ((128, LANES), BF),
    ((8, LANES), F32),
)


def front(late, pieces, gain, proj, projT, outw, bias, row):
    consts = (gain, proj, projT, outw, bias)
    shapes = [(4, 14, 28, 128)] if late else [(4, 9, 28, 128), (4, 5, 28, 128)]
    out = pl.pallas_call(
        functools.partial(front_kernel, late),
        grid=(STEPS,),
        in_specs=[whole(a.shape) for a in tuple(pieces) + consts] + [each((1, LANES))],
        out_specs=[whole(s) for s in shapes] + [each(s) for s, _ in SAVED],
        out_shape=[jax.ShapeDtypeStruct(s, BF) for s in shapes]
        + [jax.ShapeDtypeStruct((8,) + s, d) for s, d in SAVED],
        scratch_shapes=[
            pltpu.VMEM((4, 14, 40, 128), F32),
            pltpu.VMEM((8, ROWS, 128), F32),
        ],
        compiler_params=params(),
    )(*pieces, *consts, row)
    return out[: len(shapes)], out[len(shapes) :]


def back_kernel(late, *refs):
    n_in = 4 if late else 2
    pieces, refs = refs[:n_in], refs[n_in:]
    gain_ref, proj_ref, outw_ref = refs[:3]
    xw_ref, kv_ref, t_ref, p_ref, o_ref, inv_ref = refs[3:9]
    refs = refs[9:]
    n_out = 4 if late else 2
    outs, refs = refs[:n_out], refs[n_out:]
    stage, win = refs
    step = pl.program_id(0)

    @pl.when(step == 0)
    def _():
        if late:
            put_rows(stage, slice(0, 4), slice(0, 14), pieces[0][...])
            outs[1][:, 11:15] = pieces[1][...]
            outs[2][:, 3:6] = pieces[2][...]
            outs[3][:, 3:6] = pieces[3][...]
        else:
            put_rows(stage, slice(0, 4), slice(0, 9), pieces[0][...])
            put_rows(stage, slice(0, 4), slice(9, 14), pieces[1][...])
        cut_windows(stage, win)

    drs, operands = [], []
    for u in range(PER_STEP):
        dr = win[step * PER_STEP + u]
        drs.append(dr)
        operands.append(
            (
                kv_ref[u, :, 128:],
                t_ref[u, :128],
                t_ref[u, 128:],
                o_ref[u].astype(F32),
                dot_nt(outw_ref[...], lengthen(dr.astype(BF))),
                inv_ref[u],
                lambda h, u=u: p_ref[u, h],
            )
        )
    for u, (dq, dk, dv) in enumerate(attend_four_back(operands)):
        dpacked = jnp.concatenate([dq.astype(BF), dk.astype(BF), dv.astype(BF)], 1)
        dn = dot_nt(dpacked, proj_ref[...])
        xhat, rstd = normalise(xw_ref[u].astype(F32))
        win[step * PER_STEP + u] = drs[u] + normalise_back(dn * gain_ref[...], xhat, rstd)

    @pl.when(step == STEPS - 1)
    def _():
        join_windows(win, stage)
        if late:
            outs[0][...] = stage[0:2, 0:11, 0:28, :].astype(BF)
            outs[1][:, 0:11] = stage[2:4, 0:11, 0:28, :].astype(BF)
            outs[2][:, 0:3] = stage[0:2, 11:14, 0:28, :].astype(BF)
            outs[3][:, 0:3] = stage[2:4, 11:14, 0:28, :].astype(BF)
        else:
            outs[0][...] = stage[0:2, :, 0:28, :].astype(BF)
            outs[1][...] = stage[2:4, :, 0:28, :].astype(BF)


def back(late, pieces, gain, proj, outw, saved):
    consts = (gain, proj, outw)
    if late:
        shapes = [(2, n, 28, 128) for n in (11, 15, 6, 6)]
    else:
        shapes = [(2, 14, 28, 128), (2, 14, 28, 128)]
    return pl.pallas_call(
        functools.partial(back_kernel, late),
        grid=(STEPS,),
        in_specs=[whole(a.shape) for a in tuple(pieces) + consts] + [each(s) for s, _ in SAVED],
        out_specs=[whole(s) for s in shapes],
        out_shape=[jax.ShapeDtypeStruct(s, BF) for s in shapes],
        scratch_shapes=[
            pltpu.VMEM((4, 14, 40, 128), F32),
            pltpu.VMEM((8, ROWS, 128), F32),
        ],
        compiler_params=params(),
    )(*pieces, *consts, *saved)


def middle_kernel(
    resA_ref, resB_ref, resN_ref, cot_ref, cta_ref, cha_ref, cdg_ref,
    mg1_ref, mg2_ref, g3_ref, row_ref, mw1_hbm, mw2_hbm, p3_hbm, bias_hbm, ow3_hbm,
    dA_ref, dB_ref, dN_ref, so_ref, sta_ref, sha_ref, sdg_ref,
    stage, stage2, xhat1, rstd1, xhat2, rstd2, cotw, k_s, v_s, qT_s, kT_s, vT_s, probs_s, oT_s, inv_s, doT_s, dqkv_s,
    mw1_ref, mw2_ref, p3_ref, bias_ref, ow3_ref, sems,
):
    fetches = [
        pltpu.make_async_copy(there, here, sems.at[i])
        for i, (there, here) in enumerate(
            (
                (mw1_hbm, mw1_ref),
                (mw2_hbm, mw2_ref),
                (p3_hbm, p3_ref),
                (bias_hbm, bias_ref),
                (ow3_hbm, ow3_ref),
            )
        )
    ]
    for fetch in fetches:
        fetch.start()
    sources = [(resA_ref, i) for i in range(5)] + [(resB_ref, i) for i in range(14)]
    sources += [(resN_ref, i) for i in range(9)]
    for i, (ref, at) in enumerate(sources):
        stage[:, i // 2, i % 2, 0:28, :] = ref[:, at].astype(F32)
    stage[:, :, :, 28:32, :] = jnp.zeros((4, 14, 2, 4, 128), F32)
    cotw[...] = jnp.zeros((4, 7, 8, 512), F32)
    cotw[0:2, 0:4, 0:7, :] = cot_ref[2:4, 3:7].astype(F32)
    cotw[2:4, 0:4, 0:7, :] = unfold(cta_ref[:, 11:15].astype(F32))
    cotw[0:2, 4:7, 0:7, :] = unfold(cha_ref[:, 3:6].astype(F32))
    cotw[2:4, 4:7, 0:7, :] = unfold(cdg_ref[:, 3:6].astype(F32))

    def merge_one(f, _):
        pieces = [
            stage[f, :, q % 2, pl.ds(q // 2, 16, stride=2), :].reshape(ROWS, 128) for q in range(4)
        ]
        xhat, rstd = normalise(jnp.concatenate(pieces, 1))
        xhat1[f] = xhat
        rstd1[f] = jnp.broadcast_to(rstd, (ROWS, 128))
        merged = dot((xhat * mg1_ref[...]).astype(BF), mw1_ref[...]).astype(BF).astype(F32)
        for half in range(2):
            stage2[half, f] = merged[:, 128 * half : 128 * half + 128].reshape(7, 2, 16, 128)
        return 0

    fetches[0].wait()
    lax.fori_loop(0, 4, merge_one, 0)
    fetches[1].wait()
    pieces = [
        stage2[half, :, :, q % 2, pl.ds(q // 2, 8, stride=2), :].reshape(ROWS, 128)
        for q in range(4)
        for half in range(2)
    ]
    xhat, rstd = normalise(jnp.concatenate(pieces, 1))
    xhat2[...] = xhat
    rstd2[...] = jnp.broadcast_to(rstd, (ROWS, 128))
    merged_two = dot((xhat * mg2_ref[...]).astype(BF), mw2_ref[...]).astype(BF).astype(F32)
    xhat3, rstd3 = normalise(merged_two)
    n3 = (xhat3 * g3_ref[...]).astype(BF)
    fetches[2].wait()
    for g in range(4):
        at = slice(128 * g, 128 * g + 128)
        q = dot(n3, p3_ref[:, 128 * g : 128 * g + 128])
        k = dot(n3, p3_ref[:, 512 + 128 * g : 640 + 128 * g])
        v = dot(n3, p3_ref[:, 1024 + 128 * g : 1152 + 128 * g])
        k_s[g] = k.astype(BF)
        v_s[g] = v.astype(BF)
        qT_s[g] = (lengthen(q).T * (SCALE * LOG2E)).astype(BF)
        kT_s[g] = lengthen(k).T.astype(BF)
        vT_s[g] = lengthen(v).T.astype(BF)
    mask = region_mask(row_ref[...])
    fetches[3].wait()

    def heads(g, _):
        def keep(h, probs):
            probs_s[g * 4 + h] = probs

        operands = (k_s[g], qT_s[g], vT_s[g], mask, lambda h: bias_ref[g * 4 + h], keep)
        ((oT_s[g], inv_s[g]),) = attend_four([operands])
        return 0

    lax.fori_loop(0, 4, heads, 0)
    fetches[4].wait()
    att = jnp.concatenate([oT_s[g].T[:ROWS].astype(BF) for g in range(4)], 1)
    mixed = dot(att, ow3_ref[...]).astype(BF).astype(F32)
    section = (merged_two + mixed).reshape(4, 7, 8, 512)
    section = fold(section[:, :, 0:7])
    so_ref[...] = section[0:2, 0:4].astype(BF)
    sta_ref[...] = section[2:4, 0:4].astype(BF)
    sha_ref[...] = section[0:2, 4:7].astype(BF)
    sdg_ref[...] = section[2:4, 4:7].astype(BF)

    cot = cotw[...].reshape(ROWS, 512)
    cot_long = lengthen(cot.astype(BF))
    for g in range(4):
        doT_s[g] = dot_nt(ow3_ref[128 * g : 128 * g + 128, :], cot_long)

    def heads_back(g, _):
        operands = (
            v_s[g], qT_s[g], kT_s[g], oT_s[g], doT_s[g], inv_s[g], lambda h: probs_s[g * 4 + h]
        )
        ((dq, dk, dv),) = attend_four_back([operands])
        dqkv_s[g] = dq.astype(BF)
        dqkv_s[4 + g] = dk.astype(BF)
        dqkv_s[8 + g] = dv.astype(BF)
        return 0

    lax.fori_loop(0, 4, heads_back, 0)
    dpacked = jnp.concatenate([dqkv_s[i] for i in range(12)], 1)
    dn3 = dot_nt(dpacked, p3_ref[...])
    dm2 = cot + normalise_back(dn3 * g3_ref[...], xhat3, rstd3)
    dn2 = dot_nt(dm2.astype(BF), mw2_ref[...])
    dg2 = normalise_back(dn2 * mg2_ref[...], xhat2[...], rstd2[:, 0:1])
    for q in range(4):
        for half in range(2):
            at = 256 * q + 128 * half
            stage2[half, :, :, q % 2, pl.ds(q // 2, 8, stride=2), :] = dg2[:, at : at + 128].reshape(
                4, 7, 8, 128
            )

    def merge_one_back(f, _):
        dm1 = jnp.concatenate([stage2[half, f].reshape(ROWS, 128) for half in range(2)], 1).astype(BF)
        dn1 = dot_nt(dm1, mw1_ref[...])
        dg1 = normalise_back(dn1 * mg1_ref[...], xhat1[f], rstd1[f, :, 0:1])
        for q in range(4):
            stage[f, :, q % 2, pl.ds(q // 2, 16, stride=2), :] = dg1[
                :, 128 * q : 128 * q + 128
            ].reshape(14, 16, 128)
        return 0

    lax.fori_loop(0, 4, merge_one_back, 0)
    targets = [(dA_ref, i) for i in range(5)] + [(dB_ref, i) for i in range(14)]
    targets += [(dN_ref, i) for i in range(9)]
    for i, (ref, at) in enumerate(targets):
        ref[:, at] = stage[:, i // 2, i % 2, 0:28, :].astype(BF)


def middle(*operands):
    shapes = [
        (4, 5, 28, 128), (4, 14, 28, 128), (4, 9, 28, 128),
        (2, 4, 28, 128), (2, 4, 28, 128), (2, 3, 28, 128), (2, 3, 28, 128),
    ]
    return pl.pallas_call(
        middle_kernel,
        in_specs=[pl.BlockSpec(memory_space=pltpu.VMEM)] * 11
        + [pl.BlockSpec(memory_space=pl.ANY)] * 5,
        out_shape=[jax.ShapeDtypeStruct(s, BF) for s in shapes],
        scratch_shapes=[
            pltpu.VMEM((4, 14, 2, 32, 128), F32),
            pltpu.VMEM((2, 4, 7, 2, 16, 128), F32),
            pltpu.VMEM((4, ROWS, 512), F32),
            pltpu.VMEM((4, ROWS, 128), F32),
            pltpu.VMEM((ROWS, 1024), F32),
            pltpu.VMEM((ROWS, 128), F32),
            pltpu.VMEM((4, 7, 8, 512), F32),
            pltpu.VMEM((4, ROWS, 128), BF),
            pltpu.VMEM((4, ROWS, 128), BF),
            pltpu.VMEM((4, 128, LANES), BF),
            pltpu.VMEM((4, 128, LANES), BF),
            pltpu.VMEM((4, 128, LANES), BF),
            pltpu.VMEM((16, ROWS, LANES), BF),
            pltpu.VMEM((4, 128, LANES), F32),
            pltpu.VMEM((4, 8, LANES), F32),
            pltpu.VMEM((4, 128, LANES), F32),
            pltpu.VMEM((12, ROWS, 128), BF),
            pltpu.VMEM((512, 256), BF),
            pltpu.VMEM((1024, 512), BF),
            pltpu.VMEM((512, 1536), BF),
            pltpu.VMEM((HEADS3, ROWS, LANES), F32),
            pltpu.VMEM((512, 512), BF),
            pltpu.SemaphoreType.DMA((5,)),
        ],
        compiler_params=params(),
    )(*operands)


def padded_ids(ids, section):
    frames, height, width = ids.shape
    if section == 3:
        ids = jnp.roll(ids, SS, 2)
    ids = ids.reshape(4, height // 7, 7, width // 7, 7)
    ids = jnp.pad(ids, ((0, 0),) * 4 + ((0, 1),), constant_values=-1)
    ids = jnp.transpose(ids, (1, 3, 0, 2, 4)).reshape(-1, ROWS)
    row = jnp.pad(ids, ((0, 0), (0, LANES - ROWS)), constant_values=-1)
    return row[:, None, :]


def send(values, axes, by):
    if len(axes) == 1:
        n = lax.axis_size(axes[0])
        pairs = [(i, (i + by) % n) for i in range(n)]
        return lax.ppermute(values, axes[0], pairs)
    n, m = lax.axis_size(axes[0]), lax.axis_size(axes[1])
    pairs = [
        (i * m + j, (i + by) % n * m + (j + by) % m) for i in range(n) for j in range(m)
    ]
    return lax.ppermute(values, axes, pairs)


def per_device(
    tokens,
    regions_one,
    regions_three,
    gain_one,
    projection_one,
    outward_one,
    table_one,
    merge_gain_one,
    merge_weight_one,
    merge_gain_two,
    merge_weight_two,
    gain_three,
    projection_three,
    outward_three,
    table_three,
    cotangent,
):
    both = ("ha", "ta")
    ta_early, ta_late, ha_late, dg_late = pack(tokens, cotangent)
    ta_early = send(ta_early, ("ta",), -1)
    ha_late = send(ha_late, ("ha",), -1)
    dg_late = send(dg_late, both, -1)
    ta_late = send(ta_late, ("ta",), -1)

    bias_one, bias_three = build_biases(table_one, table_three)
    row_one = padded_ids(regions_one, 1)
    row_three = padded_ids(regions_three, 3)
    gain = gain_one[None]
    projT = jnp.transpose(projection_one)

    args = (gain, projection_one, projT, outward_one, bias_one)
    (res_send, res_a), saved_a = front(False, (tokens, ta_early), *args, row_one[:8])
    res_next = send(res_send, ("ha",), -1)
    (res_b,), saved_b = front(True, (tokens, ta_late, ha_late, dg_late), *args, row_one[8:])
    d_a, d_b, d_send, sec_own, sec_ta, sec_ha, sec_dg = middle(
        res_a, res_b, res_next, cotangent, ta_late, ha_late, dg_late,
        merge_gain_one[None], merge_gain_two[None], gain_three[None], row_three[0],
        merge_weight_one, merge_weight_two, projection_three, bias_three, outward_three,
    )
    d_prev = send(d_send, ("ha",), 1)
    own_b, ta_b, ha_b, dg_b = back(
        True, (d_b, sec_ta, sec_ha, sec_dg), gain, projection_one, outward_one, saved_b
    )
    d_prev, own_b = lax.optimization_barrier((d_prev, own_b))
    ta_b = send(ta_b, ("ta",), 1)
    ha_b = send(ha_b, ("ha",), 1)
    dg_b = send(dg_b, both, 1)
    own_a, ta_a = back(False, (d_prev, d_a), gain, projection_one, outward_one, saved_a)
    ta_a = send(ta_a, ("ta",), 1)

    def join(corner, side, rest):
        return jnp.concatenate(
            [jnp.concatenate([corner] + side, 1), jnp.concatenate(rest, 1)], 0
        )

    section = join(dg_b[:, 3:], [ta_b[:, 11:]], [ha_b[:, 3:], sec_own])
    section = jnp.transpose(section.reshape(4, 7, 4, 7, 128), (0, 1, 3, 2, 4)).reshape(4, 7, 7, 512)
    grad = join(dg_b[:, :3], [ta_a, ta_b[:, :11]], [ha_b[:, :3], own_a, own_b])
    return (section, grad)


def solution(mesh):
    tile = P(("col", "ta"), "ha", None, None)
    ids = P(("col", "ta"), "ha", None)
    in_specs = (tile, ids, ids) + (P(),) * 12 + (tile,)
    return jax.shard_map(
        per_device, mesh=mesh, in_specs=in_specs, out_specs=(tile, tile), check_vma=False
    )
```

profile of v0, /device:TPU:0, one launch (start us, length us, event | category | flops | bytes accessed | tf_op | source)
XLA Modules:
  0.0 118.9 jit_solution(12158001325148047268)
XLA Ops:
  0.6 2.2 %copy.46.tok_ref.refs_0_ = bf16[4,28,28,128]{3,2,1,0:T(8,128)(2,1)} copy(bf16[4,28,28,128]{3,0,2,1:T(4,128)(2,1)} %param.18) | data formatting | bytes 1605632 | tf_op args[0]
  2.9 1.7 %copy.43.cot_ref = bf16[4,7,7,512]{3,2,1,0:T(8,128)(2,1)} copy(bf16[4,7,7,512]{3,0,2,1:T(4,128)(2,1)} %param.33) | data formatting | bytes 401408 | tf_op args[15]
  4.6 2.1 %shard_map.185 = (bf16[2,14,28,128]{3,2,1,0:T(8,128)(2,1)}, bf16[2,15,28,128]{3,2,1,0:T(8,128)(2,1)}, bf16[2,6,28,128]{3,2,1,0:T(8,128)(2,1)}, bf16[2,6,28,128]{3,2,1,0:T(8,128)(2,1)}) custom-call(bf16[4,28,28,128]{3,2,1,0:T(8,128)(2,1)} %copy.46.tok_ref.refs_0_, bf16[4,7,7,512]{3,2,1,0:T(8,128)(2,1)} %copy.43.cot_ref), custom_call_target="tpu_custom_call" | custom-call | tf_op jit(solution)/shard_map/pallas_call | solution.py:217
  6.7 3.0 %collective-permute-start = (bf16[2,14,28,128]{3,2,1,0:T(8,128)(2,1)}, bf16[2,14,28,128]{3,2,1,0:T(8,128)(2,1)S(1)}, u32[]{:S(2)}, u32[]{:S(2)}) collective-permute-start(bf16[2,14,28,128]{3,2,1,0:T(8,128)(2,1)} %get-tuple-element.38), channel_id=1, source_target_pairs={{0,2},{2,0},{1,3},{3,1},{4,6},{6,4},{5,7},{7,5},{8,10},{10,8},{9,1... | collective-permute-start | bytes 602120 | tf_op jit(solution)/shard_map/ppermute | solution.py:613
  9.7 1.6 %copy.44 = bf16[128,384]{0,1:T(8,128)(2,1)} copy(bf16[128,384]{1,0:T(8,128)(2,1)} %refs_3_.3) | data formatting | bytes 196608 | tf_op args[4]
  12.0 0.9 multiply_bitcast_fusion
  15.2 9.2 %shard_map.186 = (f32[4,224,256]{2,1,0:T(8,128)}, f32[16,224,256]{2,1,0:T(8,128)}) custom-call(f32[4,1280]{1,0:T(4,128)} %pad.24.t1_ref, f32[16,1280]{1,0:T(8,128)} %pad.25.t3_ref, bf16[512,256]{1,0:T(8,128)(2,1)} %constant.12.clone.s1_ref, bf16[512,256]{1,0:T(8,128)(2,1)} %constant.13.clone.s3_ref), custom_call_target="tpu_custom_call" | custom-call | tf_op jit(solution)/shard_map/pallas_call | solution.py:187
  25.1 9.1 %shard_map.187 = (bf16[4,9,28,128]{3,2,1,0:T(8,128)(2,1)}, bf16[4,5,28,128]{3,2,1,0:T(8,128)(2,1)}, bf16[8,224,128]{2,1,0:T(8,128)(2,1)}, bf16[8,224,256]{2,1,0:...) custom-call(bf16[4,28,28,128]{3,2,1,0:T(8,128)(2,1)} %copy.46.tok_re, ...), custom_call_target="tpu_custom_call" | custom-call | tf_op jit(solution)/shard_map/pallas_call | solution.py:330
  34.2 4.6 %collective-permute-start.4 = (bf16[4,9,28,128]{3,2,1,0:T(8,128)(2,1)}, bf16[4,9,28,128]{3,2,1,0:T(8,128)(2,1)S(1)}, u32[]{:S(2)}, u32[]{:S(2)}) collective-permute-start(bf16[4,9,28,128]{3,2,1,0:T(8,128)(2,1)} %get-tuple-element.45), channel_id=1, source_target_pairs={{0,28},{4,0},{8,4},{12,8},{16,12},{20,16},{24,20},{28,24},{1,29},{... | collective-permute-start | bytes 774152 | tf_op jit(solution)/shard_map/ppermute | solution.py:613
  39.9 2.3 %collective-permute-start.3 = (bf16[2,6,28,128]{3,2,1,0:T(8,128)(2,1)S(1)}, bf16[2,6,28,128]{3,2,1,0:T(8,128)(2,1)S(1)}, u32[]{:S(2)}, u32[]{:S(2)}) collective-permute-start(bf16[2,6,28,128]{3,2,1,0:T(8,128)(2,1)S(1)} %copy-done.12), channel_id=1, source_target_pairs={{0,30},{2,28},{4,2},{6,0},{8,6},{10,4},{12,10},{14,8},{16,14},{18,... | collective-permute-start | bytes 258056 | tf_op jit(solution)/shard_map/ppermute | solution.py:618
  43.7 4.5 %collective-permute-done.2.refs_2_.cha_ref = bf16[2,6,28,128]{3,2,1,0:T(8,128)(2,1)S(1)} collective-permute-done((bf16[2,6,28,128]{3,2,1,0:T(8,128)(2,1)S(1)}, bf16[2,6,28,128]{3,2,1,0:T(8,128)(2,1)S(1)}, u32[]{:S(2)}, u32[]{:S(2)}) %collective-permute-start.2) | collective-permute-done | bytes 86048 | tf_op jit(solution)/shard_map/ppermute | solution.py:613
  48.2 1.1 collective-permute-done.3.refs_3_.cdg_ref
  50.5 9.3 %shard_map.188 = (bf16[4,14,28,128]{3,2,1,0:T(8,128)(2,1)}, bf16[8,224,128]{2,1,0:T(8,128)(2,1)}, bf16[8,224,256]{2,1,0:T(8,128)(2,1)}, bf16[8,256,256]{2,1,0:T(...) custom-call(bf16[4,28,28,128]{3,2,1,0:T(8,128)(2,1)} %copy.46.tok_ref.refs_0_, ...), custom_call_target="tpu_custom_call" | custom-call | tf_op jit(solution)/shard_map/pallas_call | solution.py:330
  60.5 14.8 %shard_map.189 = (bf16[4,5,28,128]{3,2,1,0:T(8,128)(2,1)}, bf16[4,14,28,128]{3,2,1,0:T(8,128)(2,1)}, bf16[4,9,28,128]{3,2,1,0:T(8,128)(2,1)}, bf16[2,4,28,128]{3...) custom-call(bf16[4,5,28,128]{3,2,1,0:T(8,128)(2,1)} %get-tuple-eleme, ...), custom_call_target="tpu_custom_call" | custom-call | tf_op jit(solution)/shard_map/pallas_call | solution.py:564
  75.3 9.8 %shard_map.190 = (bf16[2,11,28,128]{3,2,1,0:T(8,128)(2,1)}, bf16[2,15,28,128]{3,2,1,0:T(8,128)(2,1)}, bf16[2,6,28,128]{3,2,1,0:T(8,128)(2,1)}, bf16[2,6,28,128]{3,2,1,0:T(8,128)(2,1)}) custom-call(bf16[4,14,28,128]{3,2,1,0:T(8,128)(2,1)} %get-tuple-element.47.refs_0_, bf16[2,4,28,128]{3,2,1,0:T(8,128)(2,1)} %get-tuple-element.48.refs_1_, ...), custom_call_target="tpu_custom_call" | custom-call | tf_op jit(solution)/shard_map/pallas_call | solution.py:409
  86.2 0.9 collective-permute-start.6
  87.0 3.0 %collective-permute-start.5 = (bf16[2,6,28,128]{3,2,1,0:T(8,128)(2,1)}, bf16[2,6,28,128]{3,2,1,0:T(8,128)(2,1)S(1)}, u32[]{:S(2)}, u32[]{:S(2)}) collective-permute-start(bf16[2,6,28,128]{3,2,1,0:T(8,128)(2,1)} %get-tuple-element.57), channel_id=1, source_target_pairs={{0,6},{2,4},{4,10},{6,8},{8,14},{10,12},{12,18},{14,16},{16,22},{1... | collective-permute-start | bytes 258056 | tf_op jit(solution)/shard_map/ppermute | solution.py:618
  90.0 4.3 %collective-permute-done.7 = bf16[2,6,28,128]{3,2,1,0:T(8,128)(2,1)S(1)} collective-permute-done((bf16[2,6,28,128]{3,2,1,0:T(8,128)(2,1)}, bf16[2,6,28,128]{3,2,1,0:T(8,128)(2,1)S(1)}, u32[]{:S(2)}, u32[]{:S(2)}) %collective-permute-start.7) | collective-permute-done | bytes 86048 | tf_op jit(solution)/shard_map/ppermute | solution.py:613
  94.3 5.4 %collective-permute-done.8.refs_0_ = bf16[4,9,28,128]{3,2,1,0:T(8,128)(2,1)S(1)} collective-permute-done((bf16[4,9,28,128]{3,2,1,0:T(8,128)(2,1)S(1)}, bf16[4,9,28,128]{3,2,1,0:T(8,128)(2,1)S(1)}, u32[]{:S(2)}, u32[]{:S(2)}) %collective-permute-start.8) | collective-permute-done | bytes 258080 | tf_op jit(solution)/shard_map/ppermute | solution.py:613
  100.4 9.7 %shard_map.191 = (bf16[2,14,28,128]{3,2,1,0:T(8,128)(2,1)}, bf16[2,14,28,128]{3,2,1,0:T(8,128)(2,1)}) custom-call(bf16[4,9,28,128]{3,2,1,0:T(8,128)(2,1)} %copy-done.3, bf16[4,5,28,128]{3,2,1,0:T(8,128)(2,1)} %get-tuple-element.64.refs_1_, f32[1,128]{1,0:T(1,128)} %bitcast.35, bf16[128,384]{1,0:T(8,128)(2,1)} %refs_3_.3, bf16[128,128]{1,0:T(8,128)(2,1)} %refs_4_.1, ...), custom_call_target="tpu_custom_call" | custom-call | tf_op jit(solution)/shard_map/pallas_call | solution.py:409
  110.1 1.0 collective-permute-start.9
  112.1 4.3 %collective-permute-done.9 = bf16[2,14,28,128]{3,2,1,0:T(8,128)(2,1)S(1)} collective-permute-done((bf16[2,14,28,128]{3,2,1,0:T(8,128)(2,1)}, bf16[2,14,28,128]{3,2,1,0:T(8,128)(2,1)S(1)}, u32[]{:S(2)}, u32[]{:S(2)}) %collective-permute-start.9) | collective-permute-done | bytes 200736 | tf_op jit(solution)/shard_map/ppermute | solution.py:613
  116.3 1.1 maximum_maximum_fusion
  117.4 1.5 %copy.53 = bf16[4,28,28,128]{3,0,2,1:T(4,128)(2,1)} copy(bf16[4,28,28,128]{3,2,1,0:T(8,128)(2,1)S(1)} %maximum_maximum_fusion) | data formatting | bytes 1605632
  (60 shorter events, 11.0 us)
Async XLA Ops:
  0.6 13.5 %copy-start.9 = (s32[4,28,28]{2,0,1:T(4,128)S(1)}, s32[4,28,28]{2,0,1:T(4,128)}, u32[]{:S(2)}) copy-start(s32[4,28,28]{2,0,1:T(4,128)} %param.19) | copy-start | bytes 37636
  2.9 39.9 %copy-start.8 = (s32[4,7,7]{2,0,1:T(4,128)S(1)}, s32[4,7,7]{2,0,1:T(4,128)}, u32[]{:S(2)}) copy-start(s32[4,7,7]{2,0,1:T(4,128)} %param.20) | copy-start | bytes 2356
  6.7 32.2 %copy-start.11 = (bf16[2,15,28,128]{3,2,1,0:T(8,128)(2,1)S(1)}, bf16[2,15,28,128]{3,2,1,0:T(8,128)(2,1)}, u32[]{:S(2)}) copy-start(bf16[2,15,28,128]{3,2,1,0:T(8,128)(2,1)} %get-tuple-element.41) | copy-start | bytes 645124
  6.7 32.7 %copy-start.13 = (bf16[2,6,28,128]{3,2,1,0:T(8,128)(2,1)S(1)}, bf16[2,6,28,128]{3,2,1,0:T(8,128)(2,1)}, u32[]{:S(2)}) copy-start(bf16[2,6,28,128]{3,2,1,0:T(8,128)(2,1)} %get-tuple-element.42) | copy-start | bytes 258052
  6.7 33.2 %copy-start.12 = (bf16[2,6,28,128]{3,2,1,0:T(8,128)(2,1)S(1)}, bf16[2,6,28,128]{3,2,1,0:T(8,128)(2,1)}, u32[]{:S(2)}) copy-start(bf16[2,6,28,128]{3,2,1,0:T(8,128)(2,1)} %get-tuple-element.43) | copy-start | bytes 258052
  6.7 17.8 %collective-permute-start = (bf16[2,14,28,128]{3,2,1,0:T(8,128)(2,1)}, bf16[2,14,28,128]{3,2,1,0:T(8,128)(2,1)S(1)}, u32[]{:S(2)}, u32[]{:S(2)}) collective-permute-start(bf16[2,14,28,128]{3,2,1,0:T(8,128)(2,1)} %get-tuple-element.38), channel_id=1, source_target_pairs={{0,2},{2,0},{1,3},{3,1},{4,6},{6,4},{5,7},{7,5},{8,10},{10,8},{9,1... | collective-permute-start | bytes 602120 | tf_op jit(solution)/shard_map/ppermute | solution.py:613
  24.4 0.7 copy-start.5
  34.2 25.6 %collective-permute-start.4 = (bf16[4,9,28,128]{3,2,1,0:T(8,128)(2,1)}, bf16[4,9,28,128]{3,2,1,0:T(8,128)(2,1)S(1)}, u32[]{:S(2)}, u32[]{:S(2)}) collective-permute-start(bf16[4,9,28,128]{3,2,1,0:T(8,128)(2,1)} %get-tuple-element.45), channel_id=1, source_target_pairs={{0,28},{4,0},{8,4},{12,8},{16,12},{20,16},{24,20},{28,24},{1,29},{... | collective-permute-start | bytes 774152 | tf_op jit(solution)/shard_map/ppermute | solution.py:613
  38.8 10.4 %collective-permute-start.1 = (bf16[2,15,28,128]{3,2,1,0:T(8,128)(2,1)S(1)}, bf16[2,15,28,128]{3,2,1,0:T(8,128)(2,1)S(1)}, u32[]{:S(2)}, u32[]{:S(2)}) collective-permute-start(bf16[2,15,28,128]{3,2,1,0:T(8,128)(2,1)S(1)} %copy-done.11), channel_id=1, source_target_pairs={{0,2},{2,0},{1,3},{3,1},{4,6},{6,4},{5,7},{7,5},{8,10},{10,8},{9,1... | collective-permute-start | bytes 645128 | tf_op jit(solution)/shard_map/ppermute | solution.py:613
  39.4 8.8 %collective-permute-start.2 = (bf16[2,6,28,128]{3,2,1,0:T(8,128)(2,1)S(1)}, bf16[2,6,28,128]{3,2,1,0:T(8,128)(2,1)S(1)}, u32[]{:S(2)}, u32[]{:S(2)}) collective-permute-start(bf16[2,6,28,128]{3,2,1,0:T(8,128)(2,1)S(1)} %copy-done.13), channel_id=1, source_target_pairs={{0,28},{4,0},{8,4},{12,8},{16,12},{20,16},{24,20},{28,24},{1,29},{... | collective-permute-start | bytes 258056 | tf_op jit(solution)/shard_map/ppermute | solution.py:613
  39.9 9.4 %collective-permute-start.3 = (bf16[2,6,28,128]{3,2,1,0:T(8,128)(2,1)S(1)}, bf16[2,6,28,128]{3,2,1,0:T(8,128)(2,1)S(1)}, u32[]{:S(2)}, u32[]{:S(2)}) collective-permute-start(bf16[2,6,28,128]{3,2,1,0:T(8,128)(2,1)S(1)} %copy-done.12), channel_id=1, source_target_pairs={{0,30},{2,28},{4,2},{6,0},{8,6},{10,4},{12,10},{14,8},{16,14},{18,... | collective-permute-start | bytes 258056 | tf_op jit(solution)/shard_map/ppermute | solution.py:618
  48.2 1.1 copy-start.1
  49.2 0.6 copy-start.2
  49.9 0.7 copy-start
  59.8 0.7 copy-start.4
  75.3 10.2 %copy-start.10 = (bf16[4,9,28,128]{3,2,1,0:T(8,128)(2,1)S(1)}, bf16[4,9,28,128]{3,2,1,0:T(8,128)(2,1)}, u32[]{:S(2)}) copy-start(bf16[4,9,28,128]{3,2,1,0:T(8,128)(2,1)} %get-tuple-element.61) | copy-start | bytes 774148
  85.1 9.1 %collective-permute-start.7 = (bf16[2,6,28,128]{3,2,1,0:T(8,128)(2,1)}, bf16[2,6,28,128]{3,2,1,0:T(8,128)(2,1)S(1)}, u32[]{:S(2)}, u32[]{:S(2)}) collective-permute-start(bf16[2,6,28,128]{3,2,1,0:T(8,128)(2,1)} %get-tuple-element.59), channel_id=1, source_target_pairs={{0,4},{4,8},{8,12},{12,16},{16,20},{20,24},{24,28},{28,0},{1,5},{5... | collective-permute-start | bytes 258056 | tf_op jit(solution)/shard_map/ppermute | solution.py:613
  85.5 14.2 %collective-permute-start.8 = (bf16[4,9,28,128]{3,2,1,0:T(8,128)(2,1)S(1)}, bf16[4,9,28,128]{3,2,1,0:T(8,128)(2,1)S(1)}, u32[]{:S(2)}, u32[]{:S(2)}) collective-permute-start(bf16[4,9,28,128]{3,2,1,0:T(8,128)(2,1)S(1)} %copy-done.10), channel_id=1, source_target_pairs={{0,4},{4,8},{8,12},{12,16},{16,20},{20,24},{24,28},{28,0},{1,5},{5... | collective-permute-start | bytes 774152 | tf_op jit(solution)/shard_map/ppermute | solution.py:613
  86.2 24.9 %collective-permute-start.6 = (bf16[2,15,28,128]{3,2,1,0:T(8,128)(2,1)}, bf16[2,15,28,128]{3,2,1,0:T(8,128)(2,1)S(1)}, u32[]{:S(2)}, u32[]{:S(2)}) collective-permute-start(bf16[2,15,28,128]{3,2,1,0:T(8,128)(2,1)} %get-tuple-element.58), channel_id=1, source_target_pairs={{0,2},{2,0},{1,3},{3,1},{4,6},{6,4},{5,7},{7,5},{8,10},{10,8},{9,1... | collective-permute-start | bytes 645128 | tf_op jit(solution)/shard_map/ppermute | solution.py:613
  87.0 24.1 %collective-permute-start.5 = (bf16[2,6,28,128]{3,2,1,0:T(8,128)(2,1)}, bf16[2,6,28,128]{3,2,1,0:T(8,128)(2,1)S(1)}, u32[]{:S(2)}, u32[]{:S(2)}) collective-permute-start(bf16[2,6,28,128]{3,2,1,0:T(8,128)(2,1)} %get-tuple-element.57), channel_id=1, source_target_pairs={{0,6},{2,4},{4,10},{6,8},{8,14},{10,12},{12,18},{14,16},{16,22},{1... | collective-permute-start | bytes 258056 | tf_op jit(solution)/shard_map/ppermute | solution.py:618
  99.7 0.7 copy-start.3
  100.4 10.7 %copy-start.7 = (bf16[2,4,28,128]{3,2,1,0:T(8,128)(2,1)S(1)}, bf16[2,4,28,128]{3,2,1,0:T(8,128)(2,1)}, u32[]{:S(2)}) copy-start(bf16[2,4,28,128]{3,2,1,0:T(8,128)(2,1)} %get-tuple-element.60) | copy-start | bytes 172036
  100.4 15.9 %copy-start.6 = (bf16[2,11,28,128]{3,2,1,0:T(8,128)(2,1)S(1)}, bf16[2,11,28,128]{3,2,1,0:T(8,128)(2,1)}, u32[]{:S(2)}) copy-start(bf16[2,11,28,128]{3,2,1,0:T(8,128)(2,1)} %get-tuple-element.73) | copy-start | bytes 473092
  110.1 6.2 %collective-permute-start.9 = (bf16[2,14,28,128]{3,2,1,0:T(8,128)(2,1)}, bf16[2,14,28,128]{3,2,1,0:T(8,128)(2,1)S(1)}, u32[]{:S(2)}, u32[]{:S(2)}) collective-permute-start(bf16[2,14,28,128]{3,2,1,0:T(8,128)(2,1)} %get-tuple-element.71), channel_id=1, source_target_pairs={{0,2},{2,0},{1,3},{3,1},{4,6},{6,4},{5,7},{7,5},{8,10},{10,8},{9,1... | collective-permute-start | bytes 602120 | tf_op jit(solution)/shard_map/ppermute | solution.py:613
where the time goes:
time: 119 us
  Pallas kernels  63.9 us (54%)
  waiting for transfers between devices  19.5 us (16%)
  starting transfers between devices  16.9 us (14%)
  local copies, waits for them, and re-layouts  15.1 us (13%)
  other arithmetic  2.82 us (2%)
    pallas_call x2, Pallas kernels, back(): pl.pallas_call(functools.partial(back_kernel, late), grid=(STEPS,), in_sp...  19.5 us
    ppermute x8, waiting for transfers between devices, send(): return lax.ppermute(values, axes[0], pairs)  18.4 us
    pallas_call x2, Pallas kernels, front(): pl.pallas_call(functools.partial(front_kernel, late), grid=(STEPS,), in_s...  18.3 us
    pallas_call x1, Pallas kernels, middle(): pl.pallas_call(middle_kernel, in_specs=[pl.BlockSpec(memory_space=pltpu.V...  14.8 us
    ppermute x8, starting transfers between devices, send(): return lax.ppermute(values, axes[0], pairs)  11.6 us
    unnamed x33, local copies, waits for them, and re-layouts  10.5 us
    pallas_call x1, Pallas kernels, build_biases(): pl.pallas_call(bias_kernel, out_shape=(jax.ShapeDtypeStruct((HEADS1, ROWS...  9.18 us
    ppermute x2, starting transfers between devices, send(): return lax.ppermute(values, axes, pairs)  5.31 us
  transfers between devices with their start and end apart: 10, of which 5 were waited for; matrix products, arithmetic and copies ran while one was open for 7% of the time, Pallas kernels for 24%

commit v1 on v0

--- a/solution.py
+++ b/solution.py
@@ -15,6 +15,7 @@
 ST = 2
 SS = 3
 EPSILON = 1e-05
+NREL = 1183
 LOG2E = 1.4426950408889634
 HEAD = 32
 SCALE = HEAD**-0.5
@@ -36,8 +37,12 @@
     return lax.dot_general(a, b, (((1,), (1,)), ((), ())), preferred_element_type=F32)
 
 
-def params(limit=60):
+def params(limit=24):
     return pltpu.CompilerParams(vmem_limit_bytes=limit * 1024 * 1024)
+
+
+def cost(us):
+    return pl.CostEstimate(flops=int(us * 1.1e9), bytes_accessed=int(us * 1e6), transcendentals=0)
 
 
 def normalise(x):
@@ -80,7 +85,7 @@
 
 
 def region_mask(row):
-    wide = jnp.broadcast_to(row.astype(F32), (128, LANES))
+    wide = jnp.broadcast_to(row, (128, LANES))
     column = wide.T[:ROWS]
     column = jnp.concatenate([column, column], 1)
     return jnp.where(column == wide[0:1], 0.0, GONE).astype(F32)
@@ -131,68 +136,115 @@
     return results
 
 
-def bias_kernel(t1_ref, t3_ref, s1_ref, s3_ref, o1_ref, o3_ref, x_ref):
-    for t_ref, s_ref, o_ref, heads, section in (
-        (t1_ref, s1_ref, o1_ref, HEADS1, 1),
-        (t3_ref, s3_ref, o3_ref, HEADS3, 3),
-    ):
-        for head in range(heads):
-            row = jnp.broadcast_to(t_ref[head : head + 1, :], (8, SPAN))
-            turned = pltpu.roll(row, 0, 1, stride=1, stride_axis=0)
-            if section == 3:
-                turned = jnp.concatenate([turned[4:7], turned[0:5]], 0)
-            x_ref[8 * head : 8 * head + 8, :] = turned
-        chosen = s_ref[...]
+def lanes_of(shape):
+    return lax.broadcasted_iota(jnp.int32, shape, 1)
+
+
+def region_rows(ids, section):
+    columns = ids.shape[1]
+    count = columns // WS
+    place = lax.broadcasted_iota(jnp.int32, (columns, LANES * count), 0)
+    lane = lanes_of((columns, LANES * count))
+    column = lane % 8
+    real = (column < WS) & (lane % LANES < ROWS)
+    if section == 3:
+        column = jnp.where(column < 3, column + 4, column - 3)
+    chosen = real & (place == lane // LANES * WS + column)
+    spread = dot(ids.astype(F32).astype(BF), chosen.astype(F32).astype(BF))
+    row = lax.broadcasted_iota(jnp.int32, spread.shape, 0)
+    lane = lanes_of(spread.shape)
+    real = (lane[:1] % 8 < WS) & (lane[:1] % LANES < ROWS)
+    rows = []
+    for hw in range(ids.shape[0] // (WT * WS)):
+        mine = lane % LANES // 8 == row % 4 * WS + row // 4 - WS * hw
+        inside = (row >= WT * WS * hw) & (row < WT * WS * (hw + 1))
+        found = jnp.sum(jnp.where(mine & inside, spread, 0.0), 0, keepdims=True)
+        found = jnp.where(real, found, -1.0)
+        rows += [found[:, LANES * ww : LANES * (ww + 1)] for ww in range(count)]
+    return rows
+
+
+def prepare_kernel(
+    t1_ref, t3_ref, s_ref, r1_ref, r3_ref, o1_ref, o3_ref, row1_ref, row3_ref, tab, spread
+):
+    tab[...] = jnp.zeros((24, SPAN), F32)
+    tab[0:4, 0:NREL] = t1_ref[...] * LOG2E
+    tab[8:24, 0:NREL] = t3_ref[...] * LOG2E
+    slabs = []
+    for dt in range(7):
+        start = 169 * dt
+        low = start // 128 * 128
+        run = tab[:, low : low + 384]
+        if start > low:
+            run = pltpu.roll(run, 384 - (start - low), 1)
+        slabs.append(run[:, :256])
+    left = jnp.concatenate(slabs, 0)
+    first = left.astype(BF)
+    rest = left - first.astype(F32)
+    second = rest.astype(BF)
+    third = (rest - second.astype(F32)).astype(BF)
+    chosen = s_ref[...]
+    got = dot(first, chosen) + dot(second, chosen) + dot(third, chosen)
+    lane16 = lanes_of((16, 128))
+    for dt in range(7):
+        for wj in range(8):
+            part = got[24 * dt : 24 * dt + 24, 128 * wj : 128 * wj + 128]
+            spread[dt, pl.ds(wj, 8, stride=8), :] = part[0:8]
+            later = part[8:24]
+            turned = jnp.where(lane16 % 8 < 3, pltpu.roll(later, 124, 1), pltpu.roll(later, 3, 1))
+            spread[dt, pl.ds(64 + (7 if wj == 7 else (wj + 3) % 7), 16, stride=8), :] = turned
+    for o_ref, heads, at in ((o1_ref, HEADS1, 0), (o3_ref, HEADS3, 64)):
+        lane = lanes_of((heads * 8, 128))
         for tj in range(WT):
-            rows = []
             for hj in range(WS):
-                slabs = []
-                for ti in range(WT):
-                    start = (ti - tj + 3) * 169 + (6 - hj) * 13 + 6
-                    low = start // 128 * 128
-                    pair = x_ref[0 : 8 * heads, low : low + 256]
-                    turn = start - low
-                    slabs.append(pltpu.roll(pair, 256 - turn, 1)[:, :128] if turn else pair[:, :128])
-                rows.append(jnp.concatenate(slabs, 1))
-            left = jnp.concatenate(rows, 0)
-            first = left.astype(BF)
-            rest = left - first.astype(F32)
-            second = rest.astype(BF)
-            third = (rest - second.astype(F32)).astype(BF)
-            got = dot(first, chosen) + dot(second, chosen) + dot(third, chosen)
-            for hj in range(WS):
-                for head in range(heads):
-                    at = (hj * heads + head) * 8
-                    o_ref[head, (tj * WS + hj) * 8 : (tj * WS + hj) * 8 + 8, :] = got[at : at + 8]
-
-
-def column_order(section):
-    return [(c + 4) % 7 if section == 3 else c for c in range(7)]
-
-
-def chooser(section):
-    chosen = np.zeros((WT * 128, LANES), np.float32)
-    for ti in range(WT):
-        for hi in range(WS):
-            for c, wi in enumerate(column_order(section)):
-                chosen[ti * 128 + 13 * hi + wi, ti * 56 + hi * 8 + c] = 1.0
+                p0, p1, p2, p3 = (
+                    pltpu.roll(
+                        spread[ti - tj + 3, at : at + heads * 8, :], (ti * 56 - (6 - hj) * 8) % 128, 1
+                    )
+                    for ti in range(WT)
+                )
+                left = jnp.where(lane < 56, p0, jnp.where(lane < 112, p1, p2))
+                right = jnp.where(lane < 40, p2, p3)
+                row = (tj * WS + hj) * 8
+                o_ref[:, row : row + 8, 0:128] = left.reshape(heads, 8, 128)
+                o_ref[:, row : row + 8, 128:256] = right.reshape(heads, 8, 128)
+    for i, found in enumerate(region_rows(r1_ref[...], 1)):
+        row1_ref[i] = found
+    row3_ref[...] = region_rows(r3_ref[...], 3)[0]
+
+
+def chooser():
+    chosen = np.zeros((256, 1024), np.float32)
+    for wj in range(WS):
+        for dh in range(13):
+            for wi in range(WS):
+                chosen[dh * 13 + wi - wj + 6, wj * 128 + dh * 8 + wi] = 1.0
     return jnp.asarray(chosen, BF)
 
 
-def widen_table(table):
-    return jnp.pad(jnp.transpose(table) * LOG2E, ((0, 0), (0, SPAN - table.shape[0])))
-
-
-def build_biases(table_one, table_three):
+def by_height(ids):
+    return jnp.transpose(ids, (1, 0, 2)).reshape(-1, ids.shape[2])
+
+
+def prepare(table_one, table_three, regions_one, regions_three):
     return pl.pallas_call(
-        bias_kernel,
+        prepare_kernel,
         out_shape=(
             jax.ShapeDtypeStruct((HEADS1, ROWS, LANES), F32),
             jax.ShapeDtypeStruct((HEADS3, ROWS, LANES), F32),
+            jax.ShapeDtypeStruct((16, 1, LANES), F32),
+            jax.ShapeDtypeStruct((1, LANES), F32),
         ),
-        scratch_shapes=[pltpu.VMEM((HEADS3 * 8, SPAN), F32)],
+        scratch_shapes=[pltpu.VMEM((24, SPAN), F32), pltpu.VMEM((7, 24 * 8, 128), F32)],
         compiler_params=params(),
-    )(widen_table(table_one), widen_table(table_three), chooser(1), chooser(3))
+        cost_estimate=cost(3),
+    )(
+        jnp.transpose(table_one),
+        jnp.transpose(table_three),
+        chooser(),
+        by_height(regions_one),
+        by_height(regions_three),
+    )
 
 
 def fold(values):
@@ -220,6 +272,7 @@
             jax.ShapeDtypeStruct((2, n, 28, 128), BF) for n in (14, 15, 6, 6)
         ],
         compiler_params=params(),
+        cost_estimate=cost(2),
     )(tokens, cotangent)
 
 
@@ -249,11 +302,11 @@
 def front_kernel(late, *refs):
     n_in = 4 if late else 2
     pieces, refs = refs[:n_in], refs[n_in:]
-    gain_ref, proj_ref, projT_ref, outw_ref, bias_ref, row_ref = refs[:6]
-    refs = refs[6:]
+    gain_ref, proj_ref, outw_ref, bias_ref, row_ref = refs[:5]
+    refs = refs[5:]
     n_out = 1 if late else 2
     outs, refs = refs[:n_out], refs[n_out:]
-    xw_ref, kv_ref, t_ref, p_ref, o_ref, inv_ref, stage, win = refs
+    xw_ref, kv_ref, t_ref, p_ref, o_ref, inv_ref, stage, win, projT = refs
     step = pl.program_id(0)
 
     @pl.when(step == 0)
@@ -267,6 +320,9 @@
         else:
             put_rows(stage, slice(0, 2), slice(0, 14), own[2:4, 3:17])
             put_rows(stage, slice(2, 4), slice(0, 14), pieces[1][...])
+        for g in range(3):
+            at = slice(128 * g, 128 * g + 128)
+            projT[at, :] = proj_ref[:, at].astype(F32).T.astype(BF)
         cut_windows(stage, win)
 
     xs, operands = [], []
@@ -278,7 +334,7 @@
         n = (xhat * gain_ref[...]).astype(BF)
         kv = dot(n, proj_ref[:, 128:]).astype(BF)
         kv_ref[u] = kv
-        t = dot_nt(projT_ref[...], lengthen(n))
+        t = dot_nt(projT[...], lengthen(n))
         qT = (t[:128] * (SCALE * LOG2E)).astype(BF)
         rest = t[128:].astype(BF)
         t_ref[u, :128] = qT
@@ -324,8 +380,8 @@
 )
 
 
-def front(late, pieces, gain, proj, projT, outw, bias, row):
-    consts = (gain, proj, projT, outw, bias)
+def front(late, pieces, gain, proj, outw, bias, row):
+    consts = (gain, proj, outw, bias)
     shapes = [(4, 14, 28, 128)] if late else [(4, 9, 28, 128), (4, 5, 28, 128)]
     out = pl.pallas_call(
         functools.partial(front_kernel, late),
@@ -337,8 +393,10 @@
         scratch_shapes=[
             pltpu.VMEM((4, 14, 40, 128), F32),
             pltpu.VMEM((8, ROWS, 128), F32),
+            pltpu.VMEM((384, 128), BF),
         ],
         compiler_params=params(),
+        cost_estimate=cost(9),
     )(*pieces, *consts, row)
     return out[: len(shapes)], out[len(shapes) :]
 
@@ -417,6 +475,7 @@
             pltpu.VMEM((8, ROWS, 128), F32),
         ],
         compiler_params=params(),
+        cost_estimate=cost(10),
     )(*pieces, *consts, *saved)
 
 
@@ -591,19 +650,9 @@
             pltpu.VMEM((512, 512), BF),
             pltpu.SemaphoreType.DMA((5,)),
         ],
-        compiler_params=params(),
+        compiler_params=params(36),
+        cost_estimate=cost(14),
     )(*operands)
-
-
-def padded_ids(ids, section):
-    frames, height, width = ids.shape
-    if section == 3:
-        ids = jnp.roll(ids, SS, 2)
-    ids = ids.reshape(4, height // 7, 7, width // 7, 7)
-    ids = jnp.pad(ids, ((0, 0),) * 4 + ((0, 1),), constant_values=-1)
-    ids = jnp.transpose(ids, (1, 3, 0, 2, 4)).reshape(-1, ROWS)
-    row = jnp.pad(ids, ((0, 0), (0, LANES - ROWS)), constant_values=-1)
-    return row[:, None, :]
 
 
 def send(values, axes, by):
@@ -643,30 +692,28 @@
     dg_late = send(dg_late, both, -1)
     ta_late = send(ta_late, ("ta",), -1)
 
-    bias_one, bias_three = build_biases(table_one, table_three)
-    row_one = padded_ids(regions_one, 1)
-    row_three = padded_ids(regions_three, 3)
-    gain = gain_one[None]
-    projT = jnp.transpose(projection_one)
-
-    args = (gain, projection_one, projT, outward_one, bias_one)
+    bias_one, bias_three, row_one, row_three = prepare(
+        table_one, table_three, regions_one, regions_three
+    )
+    args = (gain_one[None], projection_one, outward_one, bias_one)
     (res_send, res_a), saved_a = front(False, (tokens, ta_early), *args, row_one[:8])
     res_next = send(res_send, ("ha",), -1)
     (res_b,), saved_b = front(True, (tokens, ta_late, ha_late, dg_late), *args, row_one[8:])
     d_a, d_b, d_send, sec_own, sec_ta, sec_ha, sec_dg = middle(
         res_a, res_b, res_next, cotangent, ta_late, ha_late, dg_late,
-        merge_gain_one[None], merge_gain_two[None], gain_three[None], row_three[0],
+        merge_gain_one[None], merge_gain_two[None], gain_three[None], row_three,
         merge_weight_one, merge_weight_two, projection_three, bias_three, outward_three,
     )
     d_prev = send(d_send, ("ha",), 1)
     own_b, ta_b, ha_b, dg_b = back(
-        True, (d_b, sec_ta, sec_ha, sec_dg), gain, projection_one, outward_one, saved_b
+        True, (d_b, sec_ta, sec_ha, sec_dg), gain_one[None], projection_one, outward_one, saved_b
     )
     d_prev, own_b = lax.optimization_barrier((d_prev, own_b))
     ta_b = send(ta_b, ("ta",), 1)
     ha_b = send(ha_b, ("ha",), 1)
     dg_b = send(dg_b, both, 1)
-    own_a, ta_a = back(False, (d_prev, d_a), gain, projection_one, outward_one, saved_a)
+    own_a, ta_a = back(False, (d_prev, d_a), gain_one[None], projection_one, outward_one, saved_a)
+    ta_b, ha_b, dg_b, own_a = lax.optimization_barrier((ta_b, ha_b, dg_b, own_a))
     ta_a = send(ta_a, ("ta",), 1)
 
     def join(corner, side, rest):

time: 119 us -> 71.7 us (0.60)
  Pallas kernels: 63.9 us -> 40.6 us
  waiting for transfers between devices: 19.5 us -> 7.02 us
  local copies, waits for them, and re-layouts: 15.1 us -> 4.76 us
  other arithmetic: 2.82 us -> 0.18 us
    ppermute x8, waiting for transfers between devices: 18.4 us -> 7.01 us  [send(): return lax.ppermute(values, axes[0], pairs)]
    unnamed x33, local copies, waits for them, and re-layouts: 10.5 us -> 3.85 us
    pallas_call x2, Pallas kernels: 18.3 us -> 11.9 us  [front(): pl.pallas_call(functools.partial(front_kernel, late), grid=(STEPS,), in_s...]
    pallas_call x1, Pallas kernels: 9.18 us -> 2.95 us  [prepare(): pl.pallas_call(prepare_kernel, out_shape=(jax.ShapeDtypeStruct((HEADS1, R...]
    pallas_call x2, Pallas kernels: 19.5 us -> 13.5 us  [back(): pl.pallas_call(functools.partial(back_kernel, late), grid=(STEPS,), in_sp...]
    ppermute x8, starting transfers between devices: 11.6 us -> 15.5 us  [send(): return lax.ppermute(values, axes[0], pairs)]
    ppermute x2, starting transfers between devices: 5.31 us -> 2.48 us  [send(): return lax.ppermute(values, axes, pairs)]
    pallas_call x1, Pallas kernels: 14.8 us -> 12.2 us  [middle(): pl.pallas_call(middle_kernel, in_specs=[pl.BlockSpec(memory_space=pltpu.V...]
  transfers between devices with their start and end apart: 10 -> 10, of which waited for: 5 -> 2; matrix products, arithmetic and copies ran while one was open for 7% -> 1% of each run, Pallas kernels for 24% -> 40%
where the time goes in v1:
time: 71.7 us; the launch traced here: 71.5 us
  Pallas kernels  40.6 us (57%)
  starting transfers between devices  18 us (25%)
  waiting for transfers between devices  7.02 us (10%)
  local copies, waits for them, and re-layouts  4.76 us (7%)
  between operations  0.99 us (1%)
    ppermute x8, starting transfers between devices, send(): return lax.ppermute(values, axes[0], pairs)  15.5 us
    pallas_call x2, Pallas kernels, back(): pl.pallas_call(functools.partial(back_kernel, late), grid=(STEPS,), in_sp...  13.5 us
    pallas_call x1, Pallas kernels, middle(): pl.pallas_call(middle_kernel, in_specs=[pl.BlockSpec(memory_space=pltpu.V...  12.2 us
    pallas_call x2, Pallas kernels, front(): pl.pallas_call(functools.partial(front_kernel, late), grid=(STEPS,), in_s...  11.9 us
    ppermute x8, waiting for transfers between devices, send(): return lax.ppermute(values, axes[0], pairs)  7.01 us
    unnamed x33, local copies, waits for them, and re-layouts  3.85 us
    pallas_call x1, Pallas kernels, prepare(): pl.pallas_call(prepare_kernel, out_shape=(jax.ShapeDtypeStruct((HEADS1, R...  2.95 us
    ppermute x2, starting transfers between devices, send(): return lax.ppermute(values, axes, pairs)  2.48 us
  transfers between devices with their start and end apart: 10, of which 2 were waited for; matrix products, arithmetic and copies ran while one was open for 1% of the time, Pallas kernels for 40%

profile of v1, /device:TPU:0, one launch (start us, length us, event | category | flops | bytes accessed | tf_op | source)
XLA Modules:
  0.0 71.5 jit_solution(4218419046099868646)
XLA Ops:
  0.6 1.0 %copy.34.cot_ref = bf16[4,7,7,512]{3,2,1,0:T(8,128)(2,1)S(1)} copy(bf16[4,7,7,512]{3,0,2,1:T(4,128)(2,1)} %param.32) | data formatting | bytes 401408 | tf_op args[15]
  1.6 1.3 %copy.35.tok_ref.refs_0_ = bf16[4,28,28,128]{3,2,1,0:T(8,128)(2,1)S(1)} copy(bf16[4,28,28,128]{3,0,2,1:T(4,128)(2,1)} %param.17) | data formatting | bytes 1605632 | tf_op args[0]
  3.0 6.1 %collective-permute-start.2 = (bf16[2,6,28,128]{3,2,1,0:T(8,128)(2,1)S(1)}, bf16[2,6,28,128]{3,2,1,0:T(8,128)(2,1)S(1)}, u32[]{:S(2)}, u32[]{:S(2)}) collective-permute-start(bf16[2,6,28,128]{3,2,1,0:T(8,128)(2,1)S(1)} %get-tuple-element.49), channel_id=1, source_target_pairs={{0,28},{4,0},{8,4},{12,8},{16,12},{20,16},{24,20},{28,24},{1,29},{... | collective-permute-start | bytes 258056 | tf_op jit(solution)/shard_map/ppermute | solution.py:662
  9.1 1.4 %collective-permute-start.3 = (bf16[2,6,28,128]{3,2,1,0:T(8,128)(2,1)S(1)}, bf16[2,6,28,128]{3,2,1,0:T(8,128)(2,1)S(1)}, u32[]{:S(2)}, u32[]{:S(2)}) collective-permute-start(bf16[2,6,28,128]{3,2,1,0:T(8,128)(2,1)S(1)} %get-tuple-element.50), channel_id=1, source_target_pairs={{0,30},{2,28},{4,2},{6,0},{8,6},{10,4},{12,10},{14,8},{16,14},{18,... | collective-permute-start | bytes 258056 | tf_op jit(solution)/shard_map/ppermute | solution.py:667
  10.5 0.5 collective-permute-start
  11.1 1.5 %collective-permute-start.1 = (bf16[2,15,28,128]{3,2,1,0:T(8,128)(2,1)S(1)}, bf16[2,15,28,128]{3,2,1,0:T(8,128)(2,1)S(1)}, u32[]{:S(2)}, u32[]{:S(2)}) collective-permute-start(bf16[2,15,28,128]{3,2,1,0:T(8,128)(2,1)S(1)} %get-tuple-element.48), channel_id=1, source_target_pairs={{0,2},{2,0},{1,3},{3,1},{4,6},{6,4},{5,7},{7,5},{8,10},{10,8},{9,1... | collective-permute-start | bytes 645128 | tf_op jit(solution)/shard_map/ppermute | solution.py:662
  12.7 3.0 %shard_map.177 = (f32[4,224,256]{2,1,0:T(8,128)S(1)}, f32[16,224,256]{2,1,0:T(8,128)S(1)}, f32[16,1,256]{2,1,0:T(1,128)S(1)}, f32[1,256]{1,0:T(1,128)S(1)}) custom-call(f32[4,1183]{1,0:T(4,128)S(1)} %bitcast.19, f32[16,1183]{1,0:T(8,128)S(1)} %bitcast.17, bf16[256,1024]{1,0:T(8,128)(2,1)S(1)} %copy-done.13, s32[112,28]{1,0:T(8,128)S(1)} %bitcast.18, ...), custom_call_target="tpu_custom_call" | custom-call | flops 3300000000 | bytes 3000000 | tf_op jit(solution)/shard_map/pallas_call | solution.py:230
  15.6 3.5 %collective-permute-done.refs_1_ = bf16[2,14,28,128]{3,2,1,0:T(8,128)(2,1)S(1)} collective-permute-done((bf16[2,14,28,128]{3,2,1,0:T(8,128)(2,1)S(1)}, bf16[2,14,28,128]{3,2,1,0:T(8,128)(2,1)S(1)}, u32[]{:S(2)}, u32[]{:S(2)}) %collective-permute-start) | collective-permute-done | bytes 200736 | tf_op jit(solution)/shard_map/ppermute | solution.py:662
  19.1 5.9 %shard_map.178 = (bf16[4,9,28,128]{3,2,1,0:T(8,128)(2,1)S(1)}, bf16[4,5,28,128]{3,2,1,0:T(8,128)(2,1)S(1)}, bf16[8,224,128]{2,1,0:T(8,128)(2,1)S(1)}, bf16[8,224...) custom-call(bf16[4,28,28,128]{3,2,1,0:T(8,128)(2,1)S(1)} %copy.35.to, ...), custom_call_target="tpu_custom_call" | custom-call | flops 9900000256 | bytes 9000000 | tf_op jit(solution)/shard_map/pallas_call | solution.py:386
  25.0 2.0 %collective-permute-start.4 = (bf16[4,9,28,128]{3,2,1,0:T(8,128)(2,1)S(1)}, bf16[4,9,28,128]{3,2,1,0:T(8,128)(2,1)S(1)}, u32[]{:S(2)}, u32[]{:S(2)}) collective-permute-start(bf16[4,9,28,128]{3,2,1,0:T(8,128)(2,1)S(1)} %get-tuple-element.52), channel_id=1, source_target_pairs={{0,28},{4,0},{8,4},{12,8},{16,12},{20,16},{24,20},{28,24},{1,29},{... | collective-permute-start | bytes 774152 | tf_op jit(solution)/shard_map/ppermute | solution.py:662
  27.2 5.9 %shard_map.179 = (bf16[4,14,28,128]{3,2,1,0:T(8,128)(2,1)S(1)}, bf16[8,224,128]{2,1,0:T(8,128)(2,1)S(1)}, bf16[8,224,256]{2,1,0:T(8,128)(2,1)S(1)}, bf16[8,256,2...) custom-call(bf16[4,28,28,128]{3,2,1,0:T(8,128)(2,1)S(1)} %copy.35.to, ...), custom_call_target="tpu_custom_call" | custom-call | flops 9900000256 | bytes 9000000 | tf_op jit(solution)/shard_map/pallas_call | solution.py:386
  33.2 12.2 %shard_map.180 = (bf16[4,5,28,128]{3,2,1,0:T(8,128)(2,1)S(1)}, bf16[4,14,28,128]{3,2,1,0:T(8,128)(2,1)S(1)}, bf16[4,9,28,128]{3,2,1,0:T(8,128)(2,1)S(1)}, bf16[2...) custom-call(bf16[4,5,28,128]{3,2,1,0:T(8,128)(2,1)S(1)} %get-tuple-e, ...), custom_call_target="tpu_custom_call" | custom-call | flops 15399999488 | bytes 14000000 | tf_op jit(solution)/shard_map/pallas_call | solution.py:623
  45.4 1.9 %collective-permute-start.8 = (bf16[4,9,28,128]{3,2,1,0:T(8,128)(2,1)S(1)}, bf16[4,9,28,128]{3,2,1,0:T(8,128)(2,1)S(1)}, u32[]{:S(2)}, u32[]{:S(2)}) collective-permute-start(bf16[4,9,28,128]{3,2,1,0:T(8,128)(2,1)S(1)} %get-tuple-element.68), channel_id=1, source_target_pairs={{0,4},{4,8},{8,12},{12,16},{16,20},{20,24},{24,28},{28,0},{1,5},{5... | collective-permute-start | bytes 774152 | tf_op jit(solution)/shard_map/ppermute | solution.py:662
  47.3 6.7 %shard_map.181 = (bf16[2,11,28,128]{3,2,1,0:T(8,128)(2,1)S(1)}, bf16[2,15,28,128]{3,2,1,0:T(8,128)(2,1)S(1)}, bf16[2,6,28,128]{3,2,1,0:T(8,128)(2,1)S(1)}, bf16[2,6,28,128]{3,2,1,0:T(8,128)(2,1)S(1)}) custom-call(bf16[4,14,28,128]{3,2,1,0:T(8,128)(2,1)S(1)} %get-tuple-element.55.refs_0_, bf16[2,4,28,128]{3,2,1,0:T(8,128)(2,1)S(1)} %get-tuple-element.56.refs_1_, ...), custom_call_target="tpu_custom_call" | custom-call | flops 11000000512 | bytes 10000000 | tf_op jit(solution)/shard_map/pallas_call | solution.py:467
  54.0 1.4 %collective-permute-start.6 = (bf16[2,6,28,128]{3,2,1,0:T(8,128)(2,1)S(1)}, bf16[2,6,28,128]{3,2,1,0:T(8,128)(2,1)S(1)}, u32[]{:S(2)}, u32[]{:S(2)}) collective-permute-start(bf16[2,6,28,128]{3,2,1,0:T(8,128)(2,1)S(1)} %get-tuple-element.66), channel_id=1, source_target_pairs={{0,4},{4,8},{8,12},{12,16},{16,20},{20,24},{24,28},{28,0},{1,5},{5... | collective-permute-start | bytes 258056 | tf_op jit(solution)/shard_map/ppermute | solution.py:662
  55.4 1.1 %collective-permute-start.7 = (bf16[2,6,28,128]{3,2,1,0:T(8,128)(2,1)S(1)}, bf16[2,6,28,128]{3,2,1,0:T(8,128)(2,1)S(1)}, u32[]{:S(2)}, u32[]{:S(2)}) collective-permute-start(bf16[2,6,28,128]{3,2,1,0:T(8,128)(2,1)S(1)} %get-tuple-element.67), channel_id=1, source_target_pairs={{0,6},{2,4},{4,10},{6,8},{8,14},{10,12},{12,18},{14,16},{16,22},{1... | collective-permute-start | bytes 258056 | tf_op jit(solution)/shard_map/ppermute | solution.py:667
  56.5 0.5 collective-permute-start.5
  57.0 6.7 %shard_map.182 = (bf16[2,14,28,128]{3,2,1,0:T(8,128)(2,1)S(1)}, bf16[2,14,28,128]{3,2,1,0:T(8,128)(2,1)S(1)}) custom-call(bf16[4,9,28,128]{3,2,1,0:T(8,128)(2,1)S(1)} %collective-permute-done.8.refs_0_, bf16[4,5,28,128]{3,2,1,0:T(8,128)(2,1)S(1)} %get-tuple-element.71.refs_1_, f32[1,128]{1,0:T(1,128)S(1)} %bitcast.26, bf16[128,384]{1,0:T(8,128)(2,1)S(1)} %copy-done.4, ...), custom_call_target="tpu_custom_call" | custom-call | flops 11000000512 | bytes 10000000 | tf_op jit(solution)/shard_map/pallas_call | solution.py:467
  63.8 1.6 %collective-permute-start.9 = (bf16[2,14,28,128]{3,2,1,0:T(8,128)(2,1)S(1)}, bf16[2,14,28,128]{3,2,1,0:T(8,128)(2,1)S(1)}, u32[]{:S(2)}, u32[]{:S(2)}) collective-permute-start(bf16[2,14,28,128]{3,2,1,0:T(8,128)(2,1)S(1)} %get-tuple-element.83), channel_id=1, source_target_pairs={{0,2},{2,0},{1,3},{3,1},{4,6},{6,4},{5,7},{7,5},{8,10},{10,8},{9,1... | collective-permute-start | bytes 602120 | tf_op jit(solution)/shard_map/ppermute | solution.py:662
  65.5 0.1 copy.38
  65.6 0.7 %copy.43 = bf16[7,4,7,1,4,128]{5,4,1,3,2,0:T(4,128)(2,1)} copy(bf16[7,4,7,1,4,128]{5,4,3,2,1,0:T(4,128)(2,1)S(1)} %bitcast.27) | data formatting | bytes 401408 | tf_op jit(solution)/shard_map/reshape | solution.py:725
  66.3 3.5 %collective-permute-done.9 = bf16[2,14,28,128]{3,2,1,0:T(8,128)(2,1)S(1)} collective-permute-done((bf16[2,14,28,128]{3,2,1,0:T(8,128)(2,1)S(1)}, bf16[2,14,28,128]{3,2,1,0:T(8,128)(2,1)S(1)}, u32[]{:S(2)}, u32[]{:S(2)}) %collective-permute-start.9) | collective-permute-done | bytes 200736 | tf_op jit(solution)/shard_map/ppermute | solution.py:662
  69.9 0.1 maximum_maximum_fusion
  70.0 1.5 %copy.40 = bf16[4,28,28,128]{3,0,2,1:T(4,128)(2,1)} copy(bf16[4,28,28,128]{3,2,1,0:T(8,128)(2,1)S(1)} %maximum_maximum_fusion) | data formatting | bytes 1605632
  (45 shorter events, 0.3 us)
Async XLA Ops:
  2.9 9.7 %copy-start.14 = (s32[4,7,7]{2,0,1:T(4,128)S(1)}, s32[4,7,7]{2,0,1:T(4,128)}, u32[]{:S(2)}) copy-start(s32[4,7,7]{2,0,1:T(4,128)} %param.19) | copy-start | bytes 2356
  2.9 9.7 %copy-start.5 = (f32[1183,16]{0,1:T(8,128)S(1)}, f32[1183,16]{0,1:T(8,128)}, u32[]{:S(2)}) copy-start(f32[1183,16]{0,1:T(8,128)} %param.31) | copy-start | bytes 227140
  2.9 9.7 %copy-start.6 = (s32[4,28,28]{2,0,1:T(4,128)S(1)}, s32[4,28,28]{2,0,1:T(4,128)}, u32[]{:S(2)}) copy-start(s32[4,28,28]{2,0,1:T(4,128)} %param.18) | copy-start | bytes 37636
  2.9 9.7 %copy-start.8 = (f32[1183,4]{0,1:T(4,128)S(1)}, f32[1183,4]{0,1:T(4,128)}, u32[]{:S(2)}) copy-start(f32[1183,4]{0,1:T(4,128)} %param.23) | copy-start | bytes 56788
  2.9 9.7 %copy-start.13 = (bf16[256,1024]{1,0:T(8,128)(2,1)S(1)}, bf16[256,1024]{1,0:T(8,128)(2,1)}, u32[]{:S(2)}) copy-start(bf16[256,1024]{1,0:T(8,128)(2,1)} %constant.2.clone.s_ref) | copy-start | bytes 1572868
  3.0 24.0 %collective-permute-start.2 = (bf16[2,6,28,128]{3,2,1,0:T(8,128)(2,1)S(1)}, bf16[2,6,28,128]{3,2,1,0:T(8,128)(2,1)S(1)}, u32[]{:S(2)}, u32[]{:S(2)}) collective-permute-start(bf16[2,6,28,128]{3,2,1,0:T(8,128)(2,1)S(1)} %get-tuple-element.49), channel_id=1, source_target_pairs={{0,28},{4,0},{8,4},{12,8},{16,12},{20,16},{24,20},{28,24},{1,29},{... | collective-permute-start | bytes 258056 | tf_op jit(solution)/shard_map/ppermute | solution.py:662
  9.1 18.0 %collective-permute-start.3 = (bf16[2,6,28,128]{3,2,1,0:T(8,128)(2,1)S(1)}, bf16[2,6,28,128]{3,2,1,0:T(8,128)(2,1)S(1)}, u32[]{:S(2)}, u32[]{:S(2)}) collective-permute-start(bf16[2,6,28,128]{3,2,1,0:T(8,128)(2,1)S(1)} %get-tuple-element.50), channel_id=1, source_target_pairs={{0,30},{2,28},{4,2},{6,0},{8,6},{10,4},{12,10},{14,8},{16,14},{18,... | collective-permute-start | bytes 258056 | tf_op jit(solution)/shard_map/ppermute | solution.py:667
  10.5 8.5 %collective-permute-start = (bf16[2,14,28,128]{3,2,1,0:T(8,128)(2,1)S(1)}, bf16[2,14,28,128]{3,2,1,0:T(8,128)(2,1)S(1)}, u32[]{:S(2)}, u32[]{:S(2)}) collective-permute-start(bf16[2,14,28,128]{3,2,1,0:T(8,128)(2,1)S(1)} %get-tuple-element.44), channel_id=1, source_target_pairs={{0,2},{2,0},{1,3},{3,1},{4,6},{6,4},{5,7},{7,5},{8,10},{10,8},{9,1... | collective-permute-start | bytes 602120 | tf_op jit(solution)/shard_map/ppermute | solution.py:662
  11.1 16.0 %collective-permute-start.1 = (bf16[2,15,28,128]{3,2,1,0:T(8,128)(2,1)S(1)}, bf16[2,15,28,128]{3,2,1,0:T(8,128)(2,1)S(1)}, u32[]{:S(2)}, u32[]{:S(2)}) collective-permute-start(bf16[2,15,28,128]{3,2,1,0:T(8,128)(2,1)S(1)} %get-tuple-element.48), channel_id=1, source_target_pairs={{0,2},{2,0},{1,3},{3,1},{4,6},{6,4},{5,7},{7,5},{8,10},{10,8},{9,1... | collective-permute-start | bytes 645128 | tf_op jit(solution)/shard_map/ppermute | solution.py:662
  12.6 6.5 %copy-start.4 = (bf16[128,384]{1,0:T(8,128)(2,1)S(1)}, bf16[128,384]{1,0:T(8,128)(2,1)}, u32[]{:S(2)}) copy-start(bf16[128,384]{1,0:T(8,128)(2,1)} %refs_3_.3) | copy-start | bytes 294916
  12.6 6.5 %copy-start.7 = (bf16[128,128]{1,0:T(8,128)(2,1)S(1)}, bf16[128,128]{1,0:T(8,128)(2,1)}, u32[]{:S(2)}) copy-start(bf16[128,128]{1,0:T(8,128)(2,1)} %refs_4_.3) | copy-start | bytes 98308
  12.6 6.4 %copy-start.12 = (f32[128]{0:T(128)S(1)}, f32[128]{0:T(128)}, u32[]{:S(2)}) copy-start(f32[128]{0:T(128)} %param.20) | copy-start | bytes 1540
  25.0 8.1 %collective-permute-start.4 = (bf16[4,9,28,128]{3,2,1,0:T(8,128)(2,1)S(1)}, bf16[4,9,28,128]{3,2,1,0:T(8,128)(2,1)S(1)}, u32[]{:S(2)}, u32[]{:S(2)}) collective-permute-start(bf16[4,9,28,128]{3,2,1,0:T(8,128)(2,1)S(1)} %get-tuple-element.52), channel_id=1, source_target_pairs={{0,28},{4,0},{8,4},{12,8},{16,12},{20,16},{24,20},{28,24},{1,29},{... | collective-permute-start | bytes 774152 | tf_op jit(solution)/shard_map/ppermute | solution.py:662
  27.1 6.0 %copy-start = (bf16[512,1536]{1,0:T(8,128)(2,1)S(1)}, bf16[512,1536]{1,0:T(8,128)(2,1)}, u32[]{:S(2)}) copy-start(bf16[512,1536]{1,0:T(8,128)(2,1)} %p3_hbm.1) | copy-start | bytes 4718596
  27.1 6.0 %copy-start.1 = (bf16[1024,512]{1,0:T(8,128)(2,1)S(1)}, bf16[1024,512]{1,0:T(8,128)(2,1)}, u32[]{:S(2)}) copy-start(bf16[1024,512]{1,0:T(8,128)(2,1)} %mw2_hbm.1) | copy-start | bytes 3145732
  27.1 6.0 %copy-start.2 = (bf16[512,512]{1,0:T(8,128)(2,1)S(1)}, bf16[512,512]{1,0:T(8,128)(2,1)}, u32[]{:S(2)}) copy-start(bf16[512,512]{1,0:T(8,128)(2,1)} %ow3_hbm.1) | copy-start | bytes 1572868
  27.1 6.0 %copy-start.3 = (bf16[512,256]{1,0:T(8,128)(2,1)S(1)}, bf16[512,256]{1,0:T(8,128)(2,1)}, u32[]{:S(2)}) copy-start(bf16[512,256]{1,0:T(8,128)(2,1)} %mw1_hbm.1) | copy-start | bytes 786436
  27.1 6.0 %copy-start.9 = (f32[1024]{0:T(1024)S(1)}, f32[1024]{0:T(1024)}, u32[]{:S(2)}) copy-start(f32[1024]{0:T(1024)} %param.26) | copy-start | bytes 12292
  27.1 6.0 %copy-start.10 = (f32[512]{0:T(512)S(1)}, f32[512]{0:T(512)}, u32[]{:S(2)}) copy-start(f32[512]{0:T(512)} %param.24) | copy-start | bytes 6148
  45.4 11.6 %collective-permute-start.8 = (bf16[4,9,28,128]{3,2,1,0:T(8,128)(2,1)S(1)}, bf16[4,9,28,128]{3,2,1,0:T(8,128)(2,1)S(1)}, u32[]{:S(2)}, u32[]{:S(2)}) collective-permute-start(bf16[4,9,28,128]{3,2,1,0:T(8,128)(2,1)S(1)} %get-tuple-element.68), channel_id=1, source_target_pairs={{0,4},{4,8},{8,12},{12,16},{16,20},{20,24},{24,28},{28,0},{1,5},{5... | collective-permute-start | bytes 774152 | tf_op jit(solution)/shard_map/ppermute | solution.py:662
  54.0 9.7 %collective-permute-start.6 = (bf16[2,6,28,128]{3,2,1,0:T(8,128)(2,1)S(1)}, bf16[2,6,28,128]{3,2,1,0:T(8,128)(2,1)S(1)}, u32[]{:S(2)}, u32[]{:S(2)}) collective-permute-start(bf16[2,6,28,128]{3,2,1,0:T(8,128)(2,1)S(1)} %get-tuple-element.66), channel_id=1, source_target_pairs={{0,4},{4,8},{8,12},{12,16},{16,20},{20,24},{24,28},{28,0},{1,5},{5... | collective-permute-start | bytes 258056 | tf_op jit(solution)/shard_map/ppermute | solution.py:662
  55.4 8.3 %collective-permute-start.7 = (bf16[2,6,28,128]{3,2,1,0:T(8,128)(2,1)S(1)}, bf16[2,6,28,128]{3,2,1,0:T(8,128)(2,1)S(1)}, u32[]{:S(2)}, u32[]{:S(2)}) collective-permute-start(bf16[2,6,28,128]{3,2,1,0:T(8,128)(2,1)S(1)} %get-tuple-element.67), channel_id=1, source_target_pairs={{0,6},{2,4},{4,10},{6,8},{8,14},{10,12},{12,18},{14,16},{16,22},{1... | collective-permute-start | bytes 258056 | tf_op jit(solution)/shard_map/ppermute | solution.py:667
  56.5 7.3 %collective-permute-start.5 = (bf16[2,15,28,128]{3,2,1,0:T(8,128)(2,1)S(1)}, bf16[2,15,28,128]{3,2,1,0:T(8,128)(2,1)S(1)}, u32[]{:S(2)}, u32[]{:S(2)}) collective-permute-start(bf16[2,15,28,128]{3,2,1,0:T(8,128)(2,1)S(1)} %get-tuple-element.65), channel_id=1, source_target_pairs={{0,2},{2,0},{1,3},{3,1},{4,6},{6,4},{5,7},{7,5},{8,10},{10,8},{9,1... | collective-permute-start | bytes 645128 | tf_op jit(solution)/shard_map/ppermute | solution.py:662
  63.8 6.1 %collective-permute-start.9 = (bf16[2,14,28,128]{3,2,1,0:T(8,128)(2,1)S(1)}, bf16[2,14,28,128]{3,2,1,0:T(8,128)(2,1)S(1)}, u32[]{:S(2)}, u32[]{:S(2)}) collective-permute-start(bf16[2,14,28,128]{3,2,1,0:T(8,128)(2,1)S(1)} %get-tuple-element.83), channel_id=1, source_target_pairs={{0,2},{2,0},{1,3},{3,1},{4,6},{6,4},{5,7},{7,5},{8,10},{10,8},{9,1... | collective-permute-start | bytes 602120 | tf_op jit(solution)/shard_map/ppermute | solution.py:662
  (1 other events, 6.0 us)

commit v2 on v1

--- a/solution.py
+++ b/solution.py
@@ -5,6 +5,7 @@
 import numpy as np
 from jax import lax
 from jax.experimental import pallas as pl
+from jax.experimental.layout import Layout, with_layout_constraint
 from jax.experimental.pallas import tpu as pltpu
 from jax.sharding import PartitionSpec as P
 
@@ -23,7 +24,7 @@
 LANES = 256
 SPAN = 1280
 GONE = -1e30
-PER_STEP = 2
+PER_STEP = 4
 STEPS = 8 // PER_STEP
 BF = jnp.bfloat16
 F32 = jnp.float32
@@ -37,7 +38,7 @@
     return lax.dot_general(a, b, (((1,), (1,)), ((), ())), preferred_element_type=F32)
 
 
-def params(limit=24):
+def params(limit=28):
     return pltpu.CompilerParams(vmem_limit_bytes=limit * 1024 * 1024)
 
 
@@ -255,25 +256,35 @@
     return jnp.concatenate([values[..., 7 * g : 7 * g + 7, :] for g in range(4)], -1)
 
 
-def pack_kernel(tok_ref, cot_ref, early_ref, late_ref, ha_ref, dg_ref):
+def early_kernel(tok_ref, early_ref):
     early_ref[...] = tok_ref[0:2, 3:17]
+
+
+def rows_kernel(tok_ref, cot_ref, ha_ref):
+    ha_ref[:, 0:3] = tok_ref[:, 0:3]
+    ha_ref[:, 3:6] = fold(cot_ref[:, 0:3].astype(F32)).astype(BF)
+
+
+def late_kernel(tok_ref, cot_ref, ha_ref, late_ref):
     late_ref[:, 0:11] = tok_ref[0:2, 17:28]
-    late_ref[:, 11:15] = fold(cot_ref[0:2, 3:7].astype(F32)).astype(BF)
-    ha_ref[:, 0:3] = tok_ref[2:4, 0:3]
-    ha_ref[:, 3:6] = fold(cot_ref[2:4, 0:3].astype(F32)).astype(BF)
-    dg_ref[:, 0:3] = tok_ref[0:2, 0:3]
-    dg_ref[:, 3:6] = fold(cot_ref[0:2, 0:3].astype(F32)).astype(BF)
-
-
-def pack(tokens, cotangent):
+    late_ref[:, 11:14] = ha_ref[0:2, 0:3]
+    late_ref[:, 14:18] = fold(cot_ref[0:2, 3:7].astype(F32)).astype(BF)
+    late_ref[:, 18:21] = ha_ref[0:2, 3:6]
+
+
+def rows_back_kernel(own_ref, ta_ref, ha_ref):
+    ha_ref[0:2, 0:3] = ta_ref[:, 11:14]
+    ha_ref[0:2, 3:6] = ta_ref[:, 18:21]
+    ha_ref[2:4] = own_ref[...]
+
+
+def arrange(kernel, shape, *operands):
     return pl.pallas_call(
-        pack_kernel,
-        out_shape=[
-            jax.ShapeDtypeStruct((2, n, 28, 128), BF) for n in (14, 15, 6, 6)
-        ],
-        compiler_params=params(),
-        cost_estimate=cost(2),
-    )(tokens, cotangent)
+        kernel,
+        out_shape=jax.ShapeDtypeStruct(shape, BF),
+        compiler_params=params(8),
+        cost_estimate=cost(0.3),
+    )(*operands)
 
 
 def put_rows(stage, frames, rows, values):
@@ -300,7 +311,7 @@
 
 
 def front_kernel(late, *refs):
-    n_in = 4 if late else 2
+    n_in = 3 if late else 2
     pieces, refs = refs[:n_in], refs[n_in:]
     gain_ref, proj_ref, outw_ref, bias_ref, row_ref = refs[:5]
     refs = refs[5:]
@@ -314,9 +325,8 @@
         own = pieces[0]
         if late:
             put_rows(stage, slice(0, 2), slice(0, 11), own[2:4, 17:28])
-            put_rows(stage, slice(2, 4), slice(0, 11), pieces[1][:, 0:11])
-            put_rows(stage, slice(0, 2), slice(11, 14), pieces[2][:, 0:3])
-            put_rows(stage, slice(2, 4), slice(11, 14), pieces[3][:, 0:3])
+            put_rows(stage, slice(2, 4), slice(0, 14), pieces[1][:, 0:14])
+            put_rows(stage, slice(0, 2), slice(11, 14), pieces[2][2:4, 0:3])
         else:
             put_rows(stage, slice(0, 2), slice(0, 14), own[2:4, 3:17])
             put_rows(stage, slice(2, 4), slice(0, 14), pieces[1][...])
@@ -402,12 +412,12 @@
 
 
 def back_kernel(late, *refs):
-    n_in = 4 if late else 2
+    n_in = 3 if late else 2
     pieces, refs = refs[:n_in], refs[n_in:]
     gain_ref, proj_ref, outw_ref = refs[:3]
     xw_ref, kv_ref, t_ref, p_ref, o_ref, inv_ref = refs[3:9]
     refs = refs[9:]
-    n_out = 4 if late else 2
+    n_out = 3 if late else 2
     outs, refs = refs[:n_out], refs[n_out:]
     stage, win = refs
     step = pl.program_id(0)
@@ -416,9 +426,8 @@
     def _():
         if late:
             put_rows(stage, slice(0, 4), slice(0, 14), pieces[0][...])
-            outs[1][:, 11:15] = pieces[1][...]
+            outs[1][:, 14:21] = pieces[1][...]
             outs[2][:, 3:6] = pieces[2][...]
-            outs[3][:, 3:6] = pieces[3][...]
         else:
             put_rows(stage, slice(0, 4), slice(0, 9), pieces[0][...])
             put_rows(stage, slice(0, 4), slice(9, 14), pieces[1][...])
@@ -450,9 +459,8 @@
         join_windows(win, stage)
         if late:
             outs[0][...] = stage[0:2, 0:11, 0:28, :].astype(BF)
-            outs[1][:, 0:11] = stage[2:4, 0:11, 0:28, :].astype(BF)
+            outs[1][:, 0:14] = stage[2:4, :, 0:28, :].astype(BF)
             outs[2][:, 0:3] = stage[0:2, 11:14, 0:28, :].astype(BF)
-            outs[3][:, 0:3] = stage[2:4, 11:14, 0:28, :].astype(BF)
         else:
             outs[0][...] = stage[0:2, :, 0:28, :].astype(BF)
             outs[1][...] = stage[2:4, :, 0:28, :].astype(BF)
@@ -461,7 +469,7 @@
 def back(late, pieces, gain, proj, outw, saved):
     consts = (gain, proj, outw)
     if late:
-        shapes = [(2, n, 28, 128) for n in (11, 15, 6, 6)]
+        shapes = [(2, n, 28, 128) for n in (11, 21, 6)]
     else:
         shapes = [(2, 14, 28, 128), (2, 14, 28, 128)]
     return pl.pallas_call(
@@ -480,9 +488,9 @@
 
 
 def middle_kernel(
-    resA_ref, resB_ref, resN_ref, cot_ref, cta_ref, cha_ref, cdg_ref,
+    resA_ref, resB_ref, resN_ref, cot_ref, cta_ref, cha_ref,
     mg1_ref, mg2_ref, g3_ref, row_ref, mw1_hbm, mw2_hbm, p3_hbm, bias_hbm, ow3_hbm,
-    dA_ref, dB_ref, dN_ref, so_ref, sta_ref, sha_ref, sdg_ref,
+    dA_ref, dB_ref, dN_ref, so_ref, sta_ref, sha_ref,
     stage, stage2, xhat1, rstd1, xhat2, rstd2, cotw, k_s, v_s, qT_s, kT_s, vT_s, probs_s, oT_s, inv_s, doT_s, dqkv_s,
     mw1_ref, mw2_ref, p3_ref, bias_ref, ow3_ref, sems,
 ):
@@ -507,9 +515,8 @@
     stage[:, :, :, 28:32, :] = jnp.zeros((4, 14, 2, 4, 128), F32)
     cotw[...] = jnp.zeros((4, 7, 8, 512), F32)
     cotw[0:2, 0:4, 0:7, :] = cot_ref[2:4, 3:7].astype(F32)
-    cotw[2:4, 0:4, 0:7, :] = unfold(cta_ref[:, 11:15].astype(F32))
-    cotw[0:2, 4:7, 0:7, :] = unfold(cha_ref[:, 3:6].astype(F32))
-    cotw[2:4, 4:7, 0:7, :] = unfold(cdg_ref[:, 3:6].astype(F32))
+    cotw[2:4, :, 0:7, :] = unfold(cta_ref[:, 14:21].astype(F32))
+    cotw[0:2, 4:7, 0:7, :] = unfold(cha_ref[2:4, 3:6].astype(F32))
 
     def merge_one(f, _):
         pieces = [
@@ -538,11 +545,9 @@
     xhat3, rstd3 = normalise(merged_two)
     n3 = (xhat3 * g3_ref[...]).astype(BF)
     fetches[2].wait()
+    packed = [dot(n3, p3_ref[:, 512 * i : 512 * i + 512]) for i in range(3)]
     for g in range(4):
-        at = slice(128 * g, 128 * g + 128)
-        q = dot(n3, p3_ref[:, 128 * g : 128 * g + 128])
-        k = dot(n3, p3_ref[:, 512 + 128 * g : 640 + 128 * g])
-        v = dot(n3, p3_ref[:, 1024 + 128 * g : 1152 + 128 * g])
+        q, k, v = (part[:, 128 * g : 128 * g + 128] for part in packed)
         k_s[g] = k.astype(BF)
         v_s[g] = v.astype(BF)
         qT_s[g] = (lengthen(q).T * (SCALE * LOG2E)).astype(BF)
@@ -551,41 +556,52 @@
     mask = region_mask(row_ref[...])
     fetches[3].wait()
 
-    def heads(g, _):
-        def keep(h, probs):
-            probs_s[g * 4 + h] = probs
-
-        operands = (k_s[g], qT_s[g], vT_s[g], mask, lambda h: bias_ref[g * 4 + h], keep)
-        ((oT_s[g], inv_s[g]),) = attend_four([operands])
+    def heads(i, _):
+        operands = []
+        for g in (2 * i, 2 * i + 1):
+
+            def keep(h, probs, g=g):
+                probs_s[g * 4 + h] = probs
+
+            operands.append(
+                (k_s[g], qT_s[g], vT_s[g], mask, lambda h, g=g: bias_ref[g * 4 + h], keep)
+            )
+        for u, (oT, inverse) in enumerate(attend_four(operands)):
+            oT_s[2 * i + u] = oT
+            inv_s[2 * i + u] = inverse
         return 0
 
-    lax.fori_loop(0, 4, heads, 0)
+    lax.fori_loop(0, 2, heads, 0)
     fetches[4].wait()
     att = jnp.concatenate([oT_s[g].T[:ROWS].astype(BF) for g in range(4)], 1)
     mixed = dot(att, ow3_ref[...]).astype(BF).astype(F32)
     section = (merged_two + mixed).reshape(4, 7, 8, 512)
     section = fold(section[:, :, 0:7])
     so_ref[...] = section[0:2, 0:4].astype(BF)
-    sta_ref[...] = section[2:4, 0:4].astype(BF)
+    sta_ref[...] = section[2:4].astype(BF)
     sha_ref[...] = section[0:2, 4:7].astype(BF)
-    sdg_ref[...] = section[2:4, 4:7].astype(BF)
 
     cot = cotw[...].reshape(ROWS, 512)
     cot_long = lengthen(cot.astype(BF))
+    doT = dot_nt(ow3_ref[...], cot_long)
     for g in range(4):
-        doT_s[g] = dot_nt(ow3_ref[128 * g : 128 * g + 128, :], cot_long)
-
-    def heads_back(g, _):
-        operands = (
-            v_s[g], qT_s[g], kT_s[g], oT_s[g], doT_s[g], inv_s[g], lambda h: probs_s[g * 4 + h]
-        )
-        ((dq, dk, dv),) = attend_four_back([operands])
-        dqkv_s[g] = dq.astype(BF)
-        dqkv_s[4 + g] = dk.astype(BF)
-        dqkv_s[8 + g] = dv.astype(BF)
+        doT_s[g] = doT[128 * g : 128 * g + 128]
+
+    def heads_back(i, _):
+        operands = [
+            (
+                v_s[g], qT_s[g], kT_s[g], oT_s[g], doT_s[g], inv_s[g],
+                lambda h, g=g: probs_s[g * 4 + h],
+            )
+            for g in (2 * i, 2 * i + 1)
+        ]
+        for u, (dq, dk, dv) in enumerate(attend_four_back(operands)):
+            dqkv_s[2 * i + u] = dq.astype(BF)
+            dqkv_s[4 + 2 * i + u] = dk.astype(BF)
+            dqkv_s[8 + 2 * i + u] = dv.astype(BF)
         return 0
 
-    lax.fori_loop(0, 4, heads_back, 0)
+    lax.fori_loop(0, 2, heads_back, 0)
     dpacked = jnp.concatenate([dqkv_s[i] for i in range(12)], 1)
     dn3 = dot_nt(dpacked, p3_ref[...])
     dm2 = cot + normalise_back(dn3 * g3_ref[...], xhat3, rstd3)
@@ -618,11 +634,11 @@
 def middle(*operands):
     shapes = [
         (4, 5, 28, 128), (4, 14, 28, 128), (4, 9, 28, 128),
-        (2, 4, 28, 128), (2, 4, 28, 128), (2, 3, 28, 128), (2, 3, 28, 128),
+        (2, 4, 28, 128), (2, 7, 28, 128), (2, 3, 28, 128),
     ]
     return pl.pallas_call(
         middle_kernel,
-        in_specs=[pl.BlockSpec(memory_space=pltpu.VMEM)] * 11
+        in_specs=[pl.BlockSpec(memory_space=pltpu.VMEM)] * 10
         + [pl.BlockSpec(memory_space=pl.ANY)] * 5,
         out_shape=[jax.ShapeDtypeStruct(s, BF) for s in shapes],
         scratch_shapes=[
@@ -655,16 +671,9 @@
     )(*operands)
 
 
-def send(values, axes, by):
-    if len(axes) == 1:
-        n = lax.axis_size(axes[0])
-        pairs = [(i, (i + by) % n) for i in range(n)]
-        return lax.ppermute(values, axes[0], pairs)
-    n, m = lax.axis_size(axes[0]), lax.axis_size(axes[1])
-    pairs = [
-        (i * m + j, (i + by) % n * m + (j + by) % m) for i in range(n) for j in range(m)
-    ]
-    return lax.ppermute(values, axes, pairs)
+def send(values, axis, by):
+    n = lax.axis_size(axis)
+    return lax.ppermute(values, axis, [(i, (i + by) % n) for i in range(n)])
 
 
 def per_device(
@@ -685,46 +694,51 @@
     table_three,
     cotangent,
 ):
-    both = ("ha", "ta")
-    ta_early, ta_late, ha_late, dg_late = pack(tokens, cotangent)
-    ta_early = send(ta_early, ("ta",), -1)
-    ha_late = send(ha_late, ("ha",), -1)
-    dg_late = send(dg_late, both, -1)
-    ta_late = send(ta_late, ("ta",), -1)
-
+    ta_early = send(arrange(early_kernel, (2, 14, 28, 128), tokens), "ta", -1)
+    ha_late = send(arrange(rows_kernel, (4, 6, 28, 128), tokens, cotangent), "ha", -1)
     bias_one, bias_three, row_one, row_three = prepare(
         table_one, table_three, regions_one, regions_three
     )
+    ta_late = send(
+        arrange(late_kernel, (2, 21, 28, 128), tokens, cotangent, ha_late), "ta", -1
+    )
     args = (gain_one[None], projection_one, outward_one, bias_one)
     (res_send, res_a), saved_a = front(False, (tokens, ta_early), *args, row_one[:8])
-    res_next = send(res_send, ("ha",), -1)
-    (res_b,), saved_b = front(True, (tokens, ta_late, ha_late, dg_late), *args, row_one[8:])
-    d_a, d_b, d_send, sec_own, sec_ta, sec_ha, sec_dg = middle(
-        res_a, res_b, res_next, cotangent, ta_late, ha_late, dg_late,
+    res_next = send(res_send, "ha", -1)
+    (res_b,), saved_b = front(True, (tokens, ta_late, ha_late), *args, row_one[8:])
+    d_a, d_b, d_send, sec_own, sec_ta, sec_ha = middle(
+        res_a, res_b, res_next, cotangent, ta_late, ha_late,
         merge_gain_one[None], merge_gain_two[None], gain_three[None], row_three,
         merge_weight_one, merge_weight_two, projection_three, bias_three, outward_three,
     )
-    d_prev = send(d_send, ("ha",), 1)
-    own_b, ta_b, ha_b, dg_b = back(
-        True, (d_b, sec_ta, sec_ha, sec_dg), gain_one[None], projection_one, outward_one, saved_b
+    d_prev = send(d_send, "ha", 1)
+    own_b, ta_b, ha_b = back(
+        True, (d_b, sec_ta, sec_ha), gain_one[None], projection_one, outward_one, saved_b
     )
     d_prev, own_b = lax.optimization_barrier((d_prev, own_b))
-    ta_b = send(ta_b, ("ta",), 1)
-    ha_b = send(ha_b, ("ha",), 1)
-    dg_b = send(dg_b, both, 1)
+    ta_b = send(ta_b, "ta", 1)
     own_a, ta_a = back(False, (d_prev, d_a), gain_one[None], projection_one, outward_one, saved_a)
-    ta_b, ha_b, dg_b, own_a = lax.optimization_barrier((ta_b, ha_b, dg_b, own_a))
-    ta_a = send(ta_a, ("ta",), 1)
-
-    def join(corner, side, rest):
-        return jnp.concatenate(
-            [jnp.concatenate([corner] + side, 1), jnp.concatenate(rest, 1)], 0
-        )
-
-    section = join(dg_b[:, 3:], [ta_b[:, 11:]], [ha_b[:, 3:], sec_own])
+    ta_b, own_a = lax.optimization_barrier((ta_b, own_a))
+    ta_a = send(ta_a, "ta", 1)
+    ha = send(arrange(rows_back_kernel, (4, 6, 28, 128), ha_b, ta_b), "ha", 1)
+
+    section = jnp.concatenate(
+        [ha[:, 3:], jnp.concatenate([ta_b[:, 14:18], sec_own], 0)], 1
+    )
     section = jnp.transpose(section.reshape(4, 7, 4, 7, 128), (0, 1, 3, 2, 4)).reshape(4, 7, 7, 512)
-    grad = join(dg_b[:, :3], [ta_a, ta_b[:, :11]], [ha_b[:, :3], own_a, own_b])
-    return (section, grad)
+    grad = jnp.concatenate(
+        [
+            ha[:, :3],
+            jnp.concatenate([jnp.zeros_like(ta_a), own_a], 0),
+            jnp.concatenate([ta_b[:, :11], own_b], 0),
+        ],
+        1,
+    )
+    in_order = Layout(major_to_minor=(0, 1, 2, 3))
+    grad = with_layout_constraint(jnp.transpose(grad, (1, 2, 0, 3)), in_order)
+    grad = lax.dynamic_update_slice(grad, jnp.transpose(ta_a, (1, 2, 0, 3)), (3, 0, 0, 0))
+    grad = with_layout_constraint(grad, in_order)
+    return (section, jnp.transpose(grad, (2, 0, 1, 3)))
 
 
 def solution(mesh):

time: 71.7 us -> 68.3 us (0.953)
  Pallas kernels: 40.6 us -> 34.3 us
  waiting for transfers between devices: 7.02 us -> 12.7 us
  starting transfers between devices: 18 us -> 13.9 us
    ppermute x10 -> x8, waiting for transfers between devices: 7.02 us -> 12.7 us  [send(): return lax.ppermute(values, axis, [(i, (i + by) % n) for i in range(n)])]
    ppermute x10 -> x8, starting transfers between devices: 18 us -> 13.9 us  [send(): return lax.ppermute(values, axis, [(i, (i + by) % n) for i in range(n)])]
    pallas_call x2, Pallas kernels: 13.5 us -> 10.9 us  [back(): pl.pallas_call(functools.partial(back_kernel, late), grid=(STEPS,), in_sp...]
    pallas_call x2, Pallas kernels: 11.9 us -> 9.39 us  [front(): pl.pallas_call(functools.partial(front_kernel, late), grid=(STEPS,), in_s...]
    pallas_call x1, Pallas kernels: 12.2 us -> 10.9 us  [middle(): pl.pallas_call(middle_kernel, in_specs=[pl.BlockSpec(memory_space=pltpu.V...]
    unnamed x33 -> x36, local copies, waits for them, and re-layouts: 3.85 us -> 3.22 us
  transfers between devices with their start and end apart: 10 -> 8, of which waited for: 2 -> 4; matrix products, arithmetic and copies ran while one was open for 1% -> 4% of each run, Pallas kernels for 40% -> 34%
where the time goes in v2:
time: 68.3 us; the launch traced here: 68.1 us
  Pallas kernels  34.3 us (50%)
  starting transfers between devices  13.9 us (20%)
  waiting for transfers between devices  12.7 us (19%)
  local copies, waits for them, and re-layouts  5.39 us (8%)
  between operations  1.04 us (2%)
  other arithmetic  0.79 us (1%)
    ppermute x8, starting transfers between devices, send(): return lax.ppermute(values, axis, [(i, (i + by) % n) for i in range(n)])  13.9 us
    ppermute x8, waiting for transfers between devices, send(): return lax.ppermute(values, axis, [(i, (i + by) % n) for i in range(n)])  12.7 us
    pallas_call x1, Pallas kernels, middle(): pl.pallas_call(middle_kernel, in_specs=[pl.BlockSpec(memory_space=pltpu.V...  10.9 us
    pallas_call x2, Pallas kernels, back(): pl.pallas_call(functools.partial(back_kernel, late), grid=(STEPS,), in_sp...  10.9 us
    pallas_call x2, Pallas kernels, front(): pl.pallas_call(functools.partial(front_kernel, late), grid=(STEPS,), in_s...  9.39 us
    unnamed x36, local copies, waits for them, and re-layouts  3.22 us
    pallas_call x1, Pallas kernels, prepare(): pl.pallas_call(prepare_kernel, out_shape=(jax.ShapeDtypeStruct((HEADS1, R...  2.96 us
  transfers between devices with their start and end apart: 8, of which 4 were waited for; matrix products, arithmetic and copies ran while one was open for 4% of the time, Pallas kernels for 34%

profile of v2, /device:TPU:0, one launch (start us, length us, event | category | flops | bytes accessed | tf_op | source)
XLA Modules:
  0.0 68.1 jit_solution(2775216004956368917)
XLA Ops:
  0.6 1.0 %copy.40.cot_ref = bf16[4,7,7,512]{3,2,1,0:T(8,128)(2,1)S(1)} copy(bf16[4,7,7,512]{3,0,2,1:T(4,128)(2,1)} %param.32) | data formatting | bytes 401408 | tf_op args[15]
  1.6 1.3 %copy.36.tok_ref.refs_0_ = bf16[4,28,28,128]{3,2,1,0:T(8,128)(2,1)S(1)} copy(bf16[4,28,28,128]{3,0,2,1:T(4,128)(2,1)} %param.17) | data formatting | bytes 1605632 | tf_op args[0]
  3.0 6.1 %collective-permute-start.1 = (bf16[4,6,28,128]{3,2,1,0:T(8,128)(2,1)S(1)}, bf16[4,6,28,128]{3,2,1,0:T(8,128)(2,1)S(1)}, u32[]{:S(2)}, u32[]{:S(2)}) collective-permute-start(bf16[4,6,28,128]{3,2,1,0:T(8,128)(2,1)S(1)} %shard_map.179), channel_id=1, source_target_pairs={{0,28},{4,0},{8,4},{12,8},{16,12},{20,16},{24,20},{28,24},{1,29},{... | collective-permute-start | bytes 516104 | tf_op jit(solution)/shard_map/ppermute | solution.py:676
  9.1 1.6 %collective-permute-start = (bf16[2,14,28,128]{3,2,1,0:T(8,128)(2,1)S(1)}, bf16[2,14,28,128]{3,2,1,0:T(8,128)(2,1)S(1)}, u32[]{:S(2)}, u32[]{:S(2)}) collective-permute-start(bf16[2,14,28,128]{3,2,1,0:T(8,128)(2,1)S(1)} %shard_map.176), channel_id=1, source_target_pairs={{0,2},{2,0},{1,3},{3,1},{4,6},{6,4},{5,7},{7,5},{8,10},{10,8},{9,1... | collective-permute-start | bytes 602120 | tf_op jit(solution)/shard_map/ppermute | solution.py:676
  10.7 3.0 %shard_map.177 = (f32[4,224,256]{2,1,0:T(8,128)S(1)}, f32[16,224,256]{2,1,0:T(8,128)S(1)}, f32[16,1,256]{2,1,0:T(1,128)S(1)}, f32[1,256]{1,0:T(1,128)S(1)}) custom-call(f32[4,1183]{1,0:T(4,128)S(1)} %bitcast.24, f32[16,1183]{1,0:T(8,128)S(1)} %bitcast.22, bf16[256,1024]{1,0:T(8,128)(2,1)S(1)} %copy-done.13, s32[112,28]{1,0:T(8,128)S(1)} %bitcast.23, ...), custom_call_target="tpu_custom_call" | custom-call | flops 3300000000 | bytes 3000000 | tf_op jit(solution)/shard_map/pallas_call | solution.py:231
  13.8 1.0 %collective-permute-start.2 = (bf16[2,21,28,128]{3,2,1,0:T(8,128)(2,1)S(1)}, bf16[2,21,28,128]{3,2,1,0:T(8,128)(2,1)S(1)}, u32[]{:S(2)}, u32[]{:S(2)}) collective-permute-start(bf16[2,21,28,128]{3,2,1,0:T(8,128)(2,1)S(1)} %shard_map.180), channel_id=1, source_target_pairs={{0,2},{2,0},{1,3},{3,1},{4,6},{6,4},{5,7},{7,5},{8,10},{10,8},{9,1... | collective-permute-start | bytes 903176 | tf_op jit(solution)/shard_map/ppermute | solution.py:676
  14.8 1.8 %collective-permute-done.refs_1_ = bf16[2,14,28,128]{3,2,1,0:T(8,128)(2,1)S(1)} collective-permute-done((bf16[2,14,28,128]{3,2,1,0:T(8,128)(2,1)S(1)}, bf16[2,14,28,128]{3,2,1,0:T(8,128)(2,1)S(1)}, u32[]{:S(2)}, u32[]{:S(2)}) %collective-permute-start) | collective-permute-done | bytes 200736 | tf_op jit(solution)/shard_map/ppermute | solution.py:676
  16.7 4.7 %shard_map.178 = (bf16[4,9,28,128]{3,2,1,0:T(8,128)(2,1)S(1)}, bf16[4,5,28,128]{3,2,1,0:T(8,128)(2,1)S(1)}, bf16[8,224,128]{2,1,0:T(8,128)(2,1)S(1)}, bf16[8,224...) custom-call(bf16[4,28,28,128]{3,2,1,0:T(8,128)(2,1)S(1)} %copy.36.to, ...), custom_call_target="tpu_custom_call" | custom-call | flops 9900000256 | bytes 9000000 | tf_op jit(solution)/shard_map/pallas_call | solution.py:396
  21.4 3.6 %collective-permute-start.3 = (bf16[4,9,28,128]{3,2,1,0:T(8,128)(2,1)S(1)}, bf16[4,9,28,128]{3,2,1,0:T(8,128)(2,1)S(1)}, u32[]{:S(2)}, u32[]{:S(2)}) collective-permute-start(bf16[4,9,28,128]{3,2,1,0:T(8,128)(2,1)S(1)} %get-tuple-element.40), channel_id=1, source_target_pairs={{0,28},{4,0},{8,4},{12,8},{16,12},{20,16},{24,20},{28,24},{1,29},{... | collective-permute-start | bytes 774152 | tf_op jit(solution)/shard_map/ppermute | solution.py:676
  25.0 4.7 %shard_map.181 = (bf16[4,14,28,128]{3,2,1,0:T(8,128)(2,1)S(1)}, bf16[8,224,128]{2,1,0:T(8,128)(2,1)S(1)}, bf16[8,224,256]{2,1,0:T(8,128)(2,1)S(1)}, bf16[8,256,2...) custom-call(bf16[4,28,28,128]{3,2,1,0:T(8,128)(2,1)S(1)} %copy.36.to, ...), custom_call_target="tpu_custom_call" | custom-call | flops 9900000256 | bytes 9000000 | tf_op jit(solution)/shard_map/pallas_call | solution.py:396
  29.7 0.4 collective-permute-done.3.resN_ref
  30.1 10.9 %shard_map.182 = (bf16[4,5,28,128]{3,2,1,0:T(8,128)(2,1)S(1)}, bf16[4,14,28,128]{3,2,1,0:T(8,128)(2,1)S(1)}, bf16[4,9,28,128]{3,2,1,0:T(8,128)(2,1)S(1)}, bf16[2...) custom-call(bf16[4,5,28,128]{3,2,1,0:T(8,128)(2,1)S(1)} %get-tuple-element.38, ...), custom_call_target="tpu_custom_call" | custom-call | flops 15399999488 | bytes 14000000 | tf_op jit(solution)/shard_map/pallas_call | solution.py:639
  41.1 0.3 collective-permute-start.5
  41.3 5.5 %shard_map.183 = (bf16[2,11,28,128]{3,2,1,0:T(8,128)(2,1)S(1)}, bf16[2,21,28,128]{3,2,1,0:T(8,128)(2,1)S(1)}, bf16[2,6,28,128]{3,2,1,0:T(8,128)(2,1)S(1)}) custom-call(bf16[4,14,28,128]{3,2,1,0:T(8,128)(2,1)S(1)} %get-tuple-element.43.refs_0_, bf16[2,7,28,128]{3,2,1,0:T(8,128)(2,1)S(1)} %get-tuple-element.44.refs_1_, ...), custom_call_target="tpu_custom_call" | custom-call | flops 11000000512 | bytes 10000000 | tf_op jit(solution)/shard_map/pallas_call | solution.py:475
  46.8 0.2 copy.43
  47.1 0.7 %collective-permute-start.4 = (bf16[2,21,28,128]{3,0,2,1:T(2,128)(2,1)S(1)}, bf16[2,21,28,128]{3,0,2,1:T(2,128)(2,1)S(1)}, u32[]{:S(2)}, u32[]{:S(2)}) collective-permute-start(bf16[2,21,28,128]{3,0,2,1:T(2,128)(2,1)S(1)} %copy.43), channel_id=1, source_target_pairs={{0,2},{2,0},{1,3},{3,1},{4,6},{6,4},{5,7},{7,5},{8,10},{10,8},{9,1... | collective-permute-start | bytes 903176 | tf_op jit(solution)/shard_map/ppermute | solution.py:676
  47.8 3.7 %collective-permute-done.5.refs_0_ = bf16[4,9,28,128]{3,2,1,0:T(8,128)(2,1)S(1)} collective-permute-done((bf16[4,9,28,128]{3,2,1,0:T(8,128)(2,1)S(1)}, bf16[4,9,28,128]{3,2,1,0:T(8,128)(2,1)S(1)}, u32[]{:S(2)}, u32[]{:S(2)}) %collective-permute-start.5) | collective-permute-done | bytes 258080 | tf_op jit(solution)/shard_map/ppermute | solution.py:676
  51.5 5.4 %shard_map.184 = (bf16[2,14,28,128]{3,2,1,0:T(8,128)(2,1)S(1)}, bf16[2,14,28,128]{3,2,1,0:T(8,128)(2,1)S(1)}) custom-call(bf16[4,9,28,128]{3,2,1,0:T(8,128)(2,1)S(1)} %collective-permute-done.5.refs_0_, bf16[4,5,28,128]{3,2,1,0:T(8,128)(2,1)S(1)} %get-tuple-element.57.refs_1_, f32[1,128]{1,0:T(1,128)S(1)} %bitcast.31, bf16[128,384]{1,0:T(8,128)(2,1)S(1)} %copy-done.4, ...), custom_call_target="tpu_custom_call" | custom-call | flops 11000000512 | bytes 10000000 | tf_op jit(solution)/shard_map/pallas_call | solution.py:475
  57.6 0.6 collective-permute-start.7
  58.5 6.8 %collective-permute-done.6 = bf16[4,6,28,128]{3,0,2,1:T(4,128)(2,1)S(1)} collective-permute-done((bf16[4,6,28,128]{3,0,2,1:T(4,128)(2,1)S(1)}, bf16[4,6,28,128]{3,0,2,1:T(4,128)(2,1)S(1)}, u32[]{:S(2)}, u32[]{:S(2)}) %collective-permute-start.6) | collective-permute-done | bytes 172064 | tf_op jit(solution)/shard_map/ppermute | solution.py:676
  65.5 0.7 %copy.53 = bf16[7,4,7,1,4,128]{5,4,1,3,2,0:T(4,128)(2,1)} copy(bf16[7,4,7,1,4,128]{5,4,3,2,1,0:T(4,128)(2,1)S(1)} %bitcast.33) | data formatting | bytes 401408 | tf_op jit(solution)/shard_map/reshape | solution.py:728
  66.3 0.6 fusion.4
  66.9 0.3 bitcast_dynamic-update-slice_fusion
  67.2 0.9 %copy-done.15 = bf16[28,28,4,128]{3,2,1,0:T(4,128)(2,1)} copy-done((bf16[28,28,4,128]{3,2,1,0:T(4,128)(2,1)}, bf16[28,28,4,128]{3,2,1,0:T(4,128)(2,1)S(1)}, u32[]{:S(2)}) %copy-start.15) | copy-done | bytes 802840
  (55 shorter events, 1.4 us)
Async XLA Ops:
  2.9 7.8 %copy-start.16 = (s32[4,7,7]{2,0,1:T(4,128)S(1)}, s32[4,7,7]{2,0,1:T(4,128)}, u32[]{:S(2)}) copy-start(s32[4,7,7]{2,0,1:T(4,128)} %param.19) | copy-start | bytes 2356
  2.9 7.8 %copy-start.5 = (f32[1183,16]{0,1:T(8,128)S(1)}, f32[1183,16]{0,1:T(8,128)}, u32[]{:S(2)}) copy-start(f32[1183,16]{0,1:T(8,128)} %param.31) | copy-start | bytes 227140
  2.9 7.7 %copy-start.6 = (s32[4,28,28]{2,0,1:T(4,128)S(1)}, s32[4,28,28]{2,0,1:T(4,128)}, u32[]{:S(2)}) copy-start(s32[4,28,28]{2,0,1:T(4,128)} %param.18) | copy-start | bytes 37636
  2.9 7.7 %copy-start.8 = (f32[1183,4]{0,1:T(4,128)S(1)}, f32[1183,4]{0,1:T(4,128)}, u32[]{:S(2)}) copy-start(f32[1183,4]{0,1:T(4,128)} %param.23) | copy-start | bytes 56788
  2.9 7.7 %copy-start.13 = (bf16[256,1024]{1,0:T(8,128)(2,1)S(1)}, bf16[256,1024]{1,0:T(8,128)(2,1)}, u32[]{:S(2)}) copy-start(bf16[256,1024]{1,0:T(8,128)(2,1)} %constant.8.clone.s_ref) | copy-start | bytes 1572868
  3.0 10.7 %collective-permute-start.1 = (bf16[4,6,28,128]{3,2,1,0:T(8,128)(2,1)S(1)}, bf16[4,6,28,128]{3,2,1,0:T(8,128)(2,1)S(1)}, u32[]{:S(2)}, u32[]{:S(2)}) collective-permute-start(bf16[4,6,28,128]{3,2,1,0:T(8,128)(2,1)S(1)} %shard_map.179), channel_id=1, source_target_pairs={{0,28},{4,0},{8,4},{12,8},{16,12},{20,16},{24,20},{28,24},{1,29},{... | collective-permute-start | bytes 516104 | tf_op jit(solution)/shard_map/ppermute | solution.py:676
  9.1 7.6 %collective-permute-start = (bf16[2,14,28,128]{3,2,1,0:T(8,128)(2,1)S(1)}, bf16[2,14,28,128]{3,2,1,0:T(8,128)(2,1)S(1)}, u32[]{:S(2)}, u32[]{:S(2)}) collective-permute-start(bf16[2,14,28,128]{3,2,1,0:T(8,128)(2,1)S(1)} %shard_map.176), channel_id=1, source_target_pairs={{0,2},{2,0},{1,3},{3,1},{4,6},{6,4},{5,7},{7,5},{8,10},{10,8},{9,1... | collective-permute-start | bytes 602120 | tf_op jit(solution)/shard_map/ppermute | solution.py:676
  13.7 3.0 %copy-start.4 = (bf16[128,384]{1,0:T(8,128)(2,1)S(1)}, bf16[128,384]{1,0:T(8,128)(2,1)}, u32[]{:S(2)}) copy-start(bf16[128,384]{1,0:T(8,128)(2,1)} %refs_3_.3) | copy-start | bytes 294916
  13.7 3.0 %copy-start.7 = (bf16[128,128]{1,0:T(8,128)(2,1)S(1)}, bf16[128,128]{1,0:T(8,128)(2,1)}, u32[]{:S(2)}) copy-start(bf16[128,128]{1,0:T(8,128)(2,1)} %refs_4_.7) | copy-start | bytes 98308
  13.7 3.0 %copy-start.12 = (f32[128]{0:T(128)S(1)}, f32[128]{0:T(128)}, u32[]{:S(2)}) copy-start(f32[128]{0:T(128)} %param.20) | copy-start | bytes 1540
  13.8 11.2 %collective-permute-start.2 = (bf16[2,21,28,128]{3,2,1,0:T(8,128)(2,1)S(1)}, bf16[2,21,28,128]{3,2,1,0:T(8,128)(2,1)S(1)}, u32[]{:S(2)}, u32[]{:S(2)}) collective-permute-start(bf16[2,21,28,128]{3,2,1,0:T(8,128)(2,1)S(1)} %shard_map.180), channel_id=1, source_target_pairs={{0,2},{2,0},{1,3},{3,1},{4,6},{6,4},{5,7},{7,5},{8,10},{10,8},{9,1... | collective-permute-start | bytes 903176 | tf_op jit(solution)/shard_map/ppermute | solution.py:676
  21.4 8.7 %collective-permute-start.3 = (bf16[4,9,28,128]{3,2,1,0:T(8,128)(2,1)S(1)}, bf16[4,9,28,128]{3,2,1,0:T(8,128)(2,1)S(1)}, u32[]{:S(2)}, u32[]{:S(2)}) collective-permute-start(bf16[4,9,28,128]{3,2,1,0:T(8,128)(2,1)S(1)} %get-tuple-element.40), channel_id=1, source_target_pairs={{0,28},{4,0},{8,4},{12,8},{16,12},{20,16},{24,20},{28,24},{1,29},{... | collective-permute-start | bytes 774152 | tf_op jit(solution)/shard_map/ppermute | solution.py:676
  25.0 5.1 %copy-start = (bf16[512,1536]{1,0:T(8,128)(2,1)S(1)}, bf16[512,1536]{1,0:T(8,128)(2,1)}, u32[]{:S(2)}) copy-start(bf16[512,1536]{1,0:T(8,128)(2,1)} %p3_hbm.1) | copy-start | bytes 4718596
  25.0 5.1 %copy-start.1 = (bf16[1024,512]{1,0:T(8,128)(2,1)S(1)}, bf16[1024,512]{1,0:T(8,128)(2,1)}, u32[]{:S(2)}) copy-start(bf16[1024,512]{1,0:T(8,128)(2,1)} %mw2_hbm.1) | copy-start | bytes 3145732
  25.0 5.1 %copy-start.2 = (bf16[512,512]{1,0:T(8,128)(2,1)S(1)}, bf16[512,512]{1,0:T(8,128)(2,1)}, u32[]{:S(2)}) copy-start(bf16[512,512]{1,0:T(8,128)(2,1)} %ow3_hbm.1) | copy-start | bytes 1572868
  25.0 5.1 %copy-start.3 = (bf16[512,256]{1,0:T(8,128)(2,1)S(1)}, bf16[512,256]{1,0:T(8,128)(2,1)}, u32[]{:S(2)}) copy-start(bf16[512,256]{1,0:T(8,128)(2,1)} %mw1_hbm.1) | copy-start | bytes 786436
  25.0 5.1 %copy-start.9 = (f32[1024]{0:T(1024)S(1)}, f32[1024]{0:T(1024)}, u32[]{:S(2)}) copy-start(f32[1024]{0:T(1024)} %param.26) | copy-start | bytes 12292
  25.0 5.1 %copy-start.10 = (f32[512]{0:T(512)S(1)}, f32[512]{0:T(512)}, u32[]{:S(2)}) copy-start(f32[512]{0:T(512)} %param.24) | copy-start | bytes 6148
  25.0 5.1 %copy-start.11 = (f32[512]{0:T(512)S(1)}, f32[512]{0:T(512)}, u32[]{:S(2)}) copy-start(f32[512]{0:T(512)} %param.28) | copy-start | bytes 6148
  41.1 10.4 %collective-permute-start.5 = (bf16[4,9,28,128]{3,2,1,0:T(8,128)(2,1)S(1)}, bf16[4,9,28,128]{3,2,1,0:T(8,128)(2,1)S(1)}, u32[]{:S(2)}, u32[]{:S(2)}) collective-permute-start(bf16[4,9,28,128]{3,2,1,0:T(8,128)(2,1)S(1)} %get-tuple-element.54), channel_id=1, source_target_pairs={{0,4},{4,8},{8,12},{12,16},{16,20},{20,24},{24,28},{28,0},{1,5},{5... | collective-permute-start | bytes 774152 | tf_op jit(solution)/shard_map/ppermute | solution.py:676
  47.1 9.8 %collective-permute-start.4 = (bf16[2,21,28,128]{3,0,2,1:T(2,128)(2,1)S(1)}, bf16[2,21,28,128]{3,0,2,1:T(2,128)(2,1)S(1)}, u32[]{:S(2)}, u32[]{:S(2)}) collective-permute-start(bf16[2,21,28,128]{3,0,2,1:T(2,128)(2,1)S(1)} %copy.43), channel_id=1, source_target_pairs={{0,2},{2,0},{1,3},{3,1},{4,6},{6,4},{5,7},{7,5},{8,10},{10,8},{9,1... | collective-permute-start | bytes 903176 | tf_op jit(solution)/shard_map/ppermute | solution.py:676
  57.1 8.2 %collective-permute-start.6 = (bf16[4,6,28,128]{3,0,2,1:T(4,128)(2,1)S(1)}, bf16[4,6,28,128]{3,0,2,1:T(4,128)(2,1)S(1)}, u32[]{:S(2)}, u32[]{:S(2)}) collective-permute-start(bf16[4,6,28,128]{3,0,2,1:T(4,128)(2,1)S(1)} %copy.45), channel_id=1, source_target_pairs={{0,4},{4,8},{8,12},{12,16},{16,20},{20,24},{24,28},{28,0},{1,5},{5... | collective-permute-start | bytes 516104 | tf_op jit(solution)/shard_map/ppermute | solution.py:676
  57.6 9.3 %collective-permute-start.7 = (bf16[2,14,28,128]{3,0,2,1:T(2,128)(2,1)S(1)}, bf16[2,14,28,128]{3,0,2,1:T(2,128)(2,1)S(1)}, u32[]{:S(2)}, u32[]{:S(2)}) collective-permute-start(bf16[2,14,28,128]{3,0,2,1:T(2,128)(2,1)S(1)} %copy.50), channel_id=1, source_target_pairs={{0,2},{2,0},{1,3},{3,1},{4,6},{6,4},{5,7},{7,5},{8,10},{10,8},{9,1... | collective-permute-start | bytes 602120 | tf_op jit(solution)/shard_map/ppermute | solution.py:676
  58.3 8.0 %slice-start = ((bf16[2,21,28,128]{3,0,2,1:T(2,128)(2,1)}), bf16[2,11,28,128]{3,0,2,1:T(2,128)(2,1)S(1)}, s32[]{:S(2)}) async-start(bf16[2,21,28,128]{3,0,2,1:T(2,128)(2,1)} %copy-done.14), calls=%async_computation | async-start | bytes 315392 | tf_op jit(solution)/shard_map/slice | solution.py:733
  (2 other events, 2.3 us)
